TPU v7x, 32 devices: a whole 2x2x4 slice. The times are simulated.
32 devices in a mesh: section: 2 (over x), tensor: 4 (over y, core), dp: 4 (over z).
Axes of the slice: x: 2, y: 2, z: 4, core: 2. Of those that a mesh axis runs over, the one named last changes fastest.
Arguments:
- tokens: bfloat16 [4, 8, 257, 1024], P(None, 'dp'), may hold values from -6 to 6
- cotangent: bfloat16 [4, 8, 257, 1024], P(None, 'dp'), may hold values from -6 to 6
- vectors: bfloat16 [2, 8, 1024], P('section'), may hold values from -0.5 to 1.5, as said below
- w_qkv: bfloat16 [2, 3, 1024, 1024], P('section', None, None, 'tensor'), may hold values from -0.1875 to 0.1875
- qv_bias: bfloat16 [2, 2, 1024], P('section', None, 'tensor'), may hold values from -2 to 2
- w_out: bfloat16 [2, 1024, 1024], P('section', 'tensor'), may hold values from -0.75 to 0.75
- w_fc1: bfloat16 [2, 1024, 4096], P('section', None, 'tensor'), may hold values from -0.1875 to 0.1875
- fc1_bias: bfloat16 [2, 4096], P('section', 'tensor'), may hold values from -2 to 2
- w_fc2: bfloat16 [2, 4096, 1024], P('section', 'tensor'), may hold values from -0.09375 to 0.09375
Outputs:
- section_outputs: bfloat16 [2, 4, 8, 257, 1024], P('section', None, 'dp')
- input_grads: float32 [2, 4, 8, 257, 1024], P('section', None, 'dp')
- grad_vectors: float32 [2, 8, 1024], P('section')
- grad_qkv: float32 [2, 3, 1024, 1024], P('section', None, None, 'tensor')
- grad_qv_bias: float32 [2, 2, 1024], P('section', None, 'tensor')
- grad_out: float32 [2, 1024, 1024], P('section', 'tensor')
- grad_fc1: float32 [2, 1024, 4096], P('section', None, 'tensor')
- grad_fc1_bias: float32 [2, 4096], P('section', 'tensor')
- grad_fc2: float32 [2, 4096, 1024], P('section', 'tensor')
Inputs may be any that keep to these rules, and one draw needn't show every extreme that they name: `vectors`: rows 0, 3, 4 and 7 of each layer lie around one, the other rows around zero.
All inputs are finite; a program needn't handle non-finite values.
Results may differ from a plain program's by a relative error of at most 0.03.
Values may be sent and summed in bfloat16 or wider, within the bound.
A program may use at most 256 MiB of HBM per device.

v0:
```python
from functools import partial

import jax
import jax.numpy as jnp
from jax import lax
from jax.sharding import PartitionSpec as P

HD = 64


eps_norm = 1e-06


def passed_along(block, axis, distance):
    devices = range(lax.axis_size(axis))
    route = [(i - distance, i) for i in devices if i - distance in devices]
    return lax.ppermute(block, axis, route)


def matmul(left, right):
    return jnp.dot(left, right, preferred_element_type=jnp.float32)


def matmul_left(left, right):
    return lax.dot_general(
        left, right, (((0,), (0,)), ((), ())), preferred_element_type=jnp.float32
    )


def matmul_right(left, right):
    return lax.dot_general(
        left, right, (((1,), (1,)), ((), ())), preferred_element_type=jnp.float32
    )


def norm_forward(values, gain, shift):
    center = values - jnp.mean(values, axis=-1, keepdims=True)
    inverse = lax.rsqrt(jnp.mean(center * center, axis=-1, keepdims=True) + eps_norm)
    unit_rows = center * inverse
    return (unit_rows * gain + shift, unit_rows, inverse)


def norm_backward(upstream, unit_rows, inverse, gain):
    scaled = upstream * gain
    inner = jnp.mean(scaled * unit_rows, axis=-1, keepdims=True)
    back = inverse * (scaled - jnp.mean(scaled, axis=-1, keepdims=True) - unit_rows * inner)
    return (back, jnp.sum(upstream * unit_rows, axis=0), jnp.sum(upstream, axis=0))


def score_block(queries, key_rows):
    return jnp.einsum(
        "bqhd,bkhd->bhqk", queries, key_rows, preferred_element_type=jnp.float32
    ) * HD ** (-0.5)


def layer_forward(token_rows, images, params):
    vector_rows, qkv_weight, bias_pair, out_weight, fc1_weight, fc1_shift, fc2_weight = params
    count_rows = token_rows.shape[0]
    col_share = qkv_weight.shape[2]
    head_shape = (images, count_rows // images, col_share // HD, HD)
    normed, unit_one, inverse_one = norm_forward(token_rows, vector_rows[0], vector_rows[1])
    normed_low = normed.astype(jnp.bfloat16)
    queries = (matmul(normed_low, qkv_weight[0]) + bias_pair[0]).astype(jnp.bfloat16)
    key_rows = matmul(normed_low, qkv_weight[1]).astype(jnp.bfloat16)
    value_rows = (matmul(normed_low, qkv_weight[2]) + bias_pair[1]).astype(jnp.bfloat16)
    scores = score_block(queries.reshape(head_shape), key_rows.reshape(head_shape))
    highest = jnp.max(scores, axis=-1, keepdims=True)
    raised = jnp.exp(scores - highest)
    totals = jnp.sum(raised, axis=-1, keepdims=True)
    probs_low = (raised / totals).astype(jnp.bfloat16)
    log_total = highest + jnp.log(totals)
    mixed = jnp.einsum(
        "bhqk,bkhd->bqhd",
        probs_low,
        value_rows.reshape(head_shape),
        preferred_element_type=jnp.float32,
    )
    mixed_low = mixed.reshape(count_rows, col_share).astype(jnp.bfloat16)
    attended = lax.psum(matmul(mixed_low, out_weight).astype(jnp.bfloat16), "tensor").astype(
        jnp.float32
    )
    after_attn = token_rows + vector_rows[3] * (attended + vector_rows[2])
    normed_two, unit_two, inverse_two = norm_forward(after_attn, vector_rows[4], vector_rows[5])
    normed_two_low = normed_two.astype(jnp.bfloat16)
    hidden_pre = matmul(normed_two_low, fc1_weight) + fc1_shift
    hidden_low = jax.nn.gelu(hidden_pre, approximate=False).astype(jnp.bfloat16)
    mlp_out = lax.psum(matmul(hidden_low, fc2_weight).astype(jnp.bfloat16), "tensor").astype(
        jnp.float32
    )
    result = after_attn + vector_rows[7] * (mlp_out + vector_rows[6])
    saved = (
        unit_one,
        inverse_one,
        normed_low,
        queries,
        key_rows,
        value_rows,
        log_total,
        mixed_low,
        attended,
        unit_two,
        inverse_two,
        normed_two_low,
        hidden_pre,
        hidden_low,
        mlp_out,
    )
    return (result, saved)


def layer_backward(upstream, images, params, kept):
    vector_rows, qkv_weight, bias_pair, out_weight, fc1_weight, fc1_shift, fc2_weight = params
    (
        unit_one,
        inverse_one,
        normed_low,
        queries,
        key_rows,
        value_rows,
        log_total,
        mixed_low,
        attended,
        unit_two,
        inverse_two,
        normed_two_low,
        hidden_pre,
        hidden_low,
        mlp_out,
    ) = kept
    count_rows, col_share = queries.shape
    head_shape = (images, count_rows // images, col_share // HD, HD)
    grad_mlp = (upstream * vector_rows[7]).astype(jnp.bfloat16)
    grad_scale_two = jnp.sum(upstream * (mlp_out + vector_rows[6]), axis=0)
    grad_bias_two = jnp.sum(upstream * vector_rows[7], axis=0)
    grad_fc2 = matmul_left(hidden_low, grad_mlp)
    grad_hidden = matmul_right(grad_mlp, fc2_weight)
    unused, gelu_back = jax.vjp(partial(jax.nn.gelu, approximate=False), hidden_pre)
    grad_pre = gelu_back(grad_hidden)[0].astype(jnp.bfloat16)
    grad_fc1_shift = jnp.sum(grad_pre.astype(jnp.float32), axis=0)
    grad_fc1 = matmul_left(normed_two_low, grad_pre)
    grad_normed_two = lax.psum(
        matmul_right(grad_pre, fc1_weight).astype(jnp.bfloat16), "tensor"
    ).astype(jnp.float32)
    back_two, grad_gain_two, grad_shift_two = norm_backward(
        grad_normed_two, unit_two, inverse_two, vector_rows[4]
    )
    grad_after = upstream + back_two
    grad_scale_one = jnp.sum(grad_after * (attended + vector_rows[2]), axis=0)
    grad_bias_one = jnp.sum(grad_after * vector_rows[3], axis=0)
    grad_attn = (grad_after * vector_rows[3]).astype(jnp.bfloat16)
    grad_outw = matmul_left(mixed_low, grad_attn)
    grad_mixed = matmul_right(grad_attn, out_weight).astype(jnp.bfloat16).reshape(head_shape)
    query_heads = queries.reshape(head_shape)
    key_heads = key_rows.reshape(head_shape)
    value_heads = value_rows.reshape(head_shape)
    probs = jnp.exp(score_block(query_heads, key_heads) - log_total)
    grad_values = jnp.einsum(
        "bhqk,bqhd->bkhd",
        probs.astype(jnp.bfloat16),
        grad_mixed,
        preferred_element_type=jnp.float32,
    )
    grad_values = grad_values.astype(jnp.bfloat16).reshape(count_rows, col_share)
    grad_probs = jnp.einsum(
        "bqhd,bkhd->bhqk", grad_mixed, value_heads, preferred_element_type=jnp.float32
    )
    grad_scores = (
        probs * (grad_probs - jnp.sum(probs * grad_probs, axis=-1, keepdims=True))
    ).astype(jnp.bfloat16)
    grad_queries = jnp.einsum(
        "bhqk,bkhd->bqhd", grad_scores, key_heads, preferred_element_type=jnp.float32
    ) * HD ** (-0.5)
    grad_queries = grad_queries.astype(jnp.bfloat16).reshape(count_rows, col_share)
    grad_keys = jnp.einsum(
        "bhqk,bqhd->bkhd", grad_scores, query_heads, preferred_element_type=jnp.float32
    ) * HD ** (-0.5)
    grad_keys = grad_keys.astype(jnp.bfloat16).reshape(count_rows, col_share)
    grad_qkv = jnp.stack(
        [
            matmul_left(normed_low, grad_queries),
            matmul_left(normed_low, grad_keys),
            matmul_left(normed_low, grad_values),
        ]
    )
    grad_pair = jnp.stack(
        [
            jnp.sum(grad_queries.astype(jnp.float32), axis=0),
            jnp.sum(grad_values.astype(jnp.float32), axis=0),
        ]
    )
    partial_normed = (
        matmul_right(grad_queries, qkv_weight[0])
        + matmul_right(grad_keys, qkv_weight[1])
        + matmul_right(grad_values, qkv_weight[2])
    )
    grad_normed = lax.psum(partial_normed.astype(jnp.bfloat16), "tensor").astype(jnp.float32)
    back_one, grad_gain_one, grad_shift_one = norm_backward(
        grad_normed, unit_one, inverse_one, vector_rows[0]
    )
    grad_vectors = jnp.stack(
        [
            grad_gain_one,
            grad_shift_one,
            grad_bias_one,
            grad_scale_one,
            grad_gain_two,
            grad_shift_two,
            grad_bias_two,
            grad_scale_two,
        ]
    )
    return (
        grad_after + back_one,
        (grad_vectors, grad_qkv, grad_pair, grad_outw, grad_fc1, grad_fc1_shift, grad_fc2),
    )


def body(tokens, cotangent, vectors, w_qkv, qv_bias, w_out, w_fc1, fc1_bias, w_fc2):
    params = (vectors[0], w_qkv[0], qv_bias[0], w_out[0], w_fc1[0], fc1_bias[0], w_fc2[0])
    micro_count, images, seq_len, model_width = tokens.shape
    count_rows = images * seq_len
    is_first = lax.axis_index("section") == 0
    arrived = jnp.zeros((count_rows, model_width), jnp.bfloat16)
    starts = []
    results = []
    records = []
    for tick_no in range(micro_count + 1):
        own_rows = tokens[min(tick_no, micro_count - 1)].reshape(count_rows, model_width)
        start_rows = jnp.where(is_first, own_rows, arrived)
        result, saved = layer_forward(start_rows.astype(jnp.float32), images, params)
        result_low = result.astype(jnp.bfloat16)
        starts.append(start_rows)
        results.append(result_low)
        records.append(saved)
        if tick_no < micro_count:
            arrived = passed_along(result_low, "section", 1)
    returned = jnp.zeros((count_rows, model_width), jnp.bfloat16)
    sums = None
    grad_rows = []
    for tick_no in range(micro_count + 1):
        late_no = min(tick_no, micro_count - 1)
        early_no = max(tick_no - 1, 0)
        incoming = jnp.where(
            is_first, returned, cotangent[late_no].reshape(count_rows, model_width)
        )
        kept = jax.tree.map(partial(jnp.where, is_first), records[early_no], records[late_no + 1])
        grad_input, terms = layer_backward(incoming.astype(jnp.float32), images, params, kept)
        weight_on = jnp.where(
            is_first, 1.0 if tick_no >= 1 else 0.0, 1.0 if tick_no < micro_count else 0.0
        )
        terms = jax.tree.map(lambda term: term * weight_on, terms)
        sums = terms if sums is None else jax.tree.map(jnp.add, sums, terms)
        grad_rows.append(grad_input)
        if tick_no < micro_count:
            returned = passed_along(grad_input.astype(jnp.bfloat16), "section", -1)
    sums = (
        lax.psum(sums[0].astype(jnp.bfloat16), "dp").astype(jnp.float32),
        lax.psum(sums[1].astype(jnp.bfloat16), "dp").astype(jnp.float32),
        lax.psum(sums[2].astype(jnp.bfloat16), "dp").astype(jnp.float32),
        lax.psum(sums[3].astype(jnp.bfloat16), "dp").astype(jnp.float32),
        lax.psum(sums[4].astype(jnp.bfloat16), "dp").astype(jnp.float32),
        lax.psum(sums[5].astype(jnp.bfloat16), "dp").astype(jnp.float32),
        lax.psum(sums[6].astype(jnp.bfloat16), "dp").astype(jnp.float32),
    )
    shape_out = (1, micro_count, images, seq_len, model_width)
    section_outputs = jnp.stack(
        [
            jnp.where(is_first, results[micro_no], results[micro_no + 1])
            for micro_no in range(micro_count)
        ]
    ).reshape(shape_out)
    input_grads = jnp.stack(
        [
            jnp.where(is_first, grad_rows[micro_no + 1], grad_rows[micro_no])
            for micro_no in range(micro_count)
        ]
    ).reshape(shape_out)
    return (
        section_outputs,
        input_grads,
        sums[0][None],
        sums[1][None],
        sums[2][None],
        sums[3][None],
        sums[4][None],
        sums[5][None],
        sums[6][None],
    )


def solution(mesh):
    return jax.shard_map(
        body,
        mesh=mesh,
        in_specs=(
            P(None, "dp", None, None),
            P(None, "dp", None, None),
            P("section", None, None),
            P("section", None, None, "tensor"),
            P("section", None, "tensor"),
            P("section", "tensor", None),
            P("section", None, "tensor"),
            P("section", "tensor"),
            P("section", "tensor", None),
        ),
        out_specs=(
            P("section", None, "dp", None, None),
            P("section", None, "dp", None, None),
            P("section", None, None),
            P("section", None, None, "tensor"),
            P("section", None, "tensor"),
            P("section", "tensor", None),
            P("section", None, "tensor"),
            P("section", "tensor"),
            P("section", "tensor", None),
        ),
        check_vma=False,
    )
```

profile of v0, /device:TPU:0, one launch (start us, length us, event | category | flops | bytes accessed | tf_op | source)
XLA Modules:
  0.0 1490.1 jit_solution(7649305300243424958)
XLA Ops:
  10.7 4.7 multiply_reduce_fusion.15
  40.0 5.6 fusion.664
  50.7 27.7 %all-reduce.24.cloned.1.call-done = bf16[514,1024]{1,0:T(8,128)(2,1)} async-done(((bf16[514,1024]{1,0:T(8,128)(2,1)}), bf16[514,1024]{1,0:T(8,128)(2,1)}) %all-reduce.24.cloned.1.call-update) | async-done | bytes 1052688 | tf_op jit(solution)/shard_map/psum | solution.py:79
  81.2 7.2 fusion.118
  91.8 36.8 %all-reduce.26.cloned.1.call-done = bf16[514,1024]{1,0:T(8,128)(2,1)} async-done(((bf16[514,1024]{1,0:T(8,128)(2,1)}), bf16[514,1024]{1,0:T(8,128)(2,1)}) %all-reduce.26.cloned.1.call-update) | async-done | bytes 1052688 | tf_op jit(solution)/shard_map/psum | solution.py:87
  131.8 4.5 collective-permute-start
  139.4 18.6 %collective-permute-done = bf16[514,1024]{1,0:T(8,128)(2,1)} collective-permute-done((bf16[514,1024]{1,0:T(8,128)(2,1)}, bf16[514,1024]{1,0:T(8,128)(2,1)}, u32[]{:S(2)}, u32[]{:S(2)}) %collective-permute-start) | collective-permute-done | bytes 1052704 | tf_op jit(solution)/shard_map/ppermute | solution.py:17
  187.4 30.4 %all-reduce.28.cloned.1.call-done = bf16[514,1024]{1,0:T(8,128)(2,1)} async-done(((bf16[514,1024]{1,0:T(8,128)(2,1)}), bf16[514,1024]{1,0:T(8,128)(2,1)}) %all-reduce.28.cloned.1.call-update) | async-done | bytes 1052688 | tf_op jit(solution)/shard_map/psum | solution.py:79
  220.4 6.2 fusion.128
  230.1 7.1 convert_reduce_fusion.18
  245.5 5.9 fusion.663
  256.6 36.7 %all-reduce.50.cloned.1.call-done = (bf16[514,1024]{1,0:T(8,128)(2,1)}, bf16[514,1024]{1,0:T(8,128)(2,1)}) async-done(((bf16[514,1024]{1,0:T(8,128)(2,1)}, bf16[514,1024]{1,0:T(8,128)(2,1)}), (bf16[514,1024]{1,0:T(8,128)(2,1)}, bf16[514,1024]{1,0:T(8,128)(2,1)})) %all-reduce.50.cloned.1.call-update) | async-done | bytes 2105360 | tf_op jit(solution)/shard_map/psum | solution.py:87
  293.2 4.5 broadcast_select_fusion.19
  297.7 4.0 collective-permute-start.1
  309.7 14.0 collective-permute-done.1
  382.6 4.0 add_convert_fusion.7
  406.4 7.0 fusion.486
  413.4 26.7 %all-reduce.48.cloned.1.call-done = (bf16[514,1024]{1,0:T(8,128)(2,1)}, bf16[514,1024]{1,0:T(8,128)(2,1)}) async-done(((bf16[514,1024]{1,0:T(8,128)(2,1)}, bf16[514,1024]{1,0:T(8,128)(2,1)}), (bf16[514,1024]{1,0:T(8,128)(2,1)}, bf16[514,1024]{1,0:T(8,128)(2,1)})) %all-reduce.48.cloned.1.call-update) | async-done | bytes 2105360 | tf_op jit(solution)/shard_map/psum | solution.py:79
  450.6 6.2 fusion.141
  459.1 17.1 %collective-permute-done.4 = bf16[514,1024]{1,0:T(8,128)(2,1)S(1)} collective-permute-done((bf16[514,1024]{1,0:T(8,128)(2,1)S(1)}, bf16[514,1024]{1,0:T(8,128)(2,1)S(1)}, u32[]{:S(2)}, u32[]{:S(2)}) %collective-permute-start.4) | collective-permute-done | bytes 1052704 | tf_op jit(solution)/shard_map/ppermute | solution.py:17
  476.3 7.0 convert_reduce_fusion.17
  487.9 5.5 fusion.469
  511.3 27.0 %all-reduce.46.cloned.1.call-done = (bf16[514,1024]{1,0:T(8,128)(2,1)}, bf16[514,1024]{1,0:T(8,128)(2,1)}) async-done(((bf16[514,1024]{1,0:T(8,128)(2,1)}, bf16[514,1024]{1,0:T(8,128)(2,1)}), (bf16[514,1024]{1,0:T(8,128)(2,1)}, bf16[514,1024]{1,0:T(8,128)(2,1)})) %all-reduce.46.cloned.1.call-update) | async-done | bytes 2105360 | tf_op jit(solution)/shard_map/psum | solution.py:87
  538.3 4.5 broadcast_select_fusion.17
  542.8 4.4 collective-permute-start.2
  552.7 4.2 convert_reduce_fusion.26
  597.2 7.4 fusion.484
  604.7 4.0 fusion.476
  613.8 34.8 %all-reduce.44.cloned.1.call-done = (bf16[514,1024]{1,0:T(8,128)(2,1)}, bf16[514,1024]{1,0:T(8,128)(2,1)}) async-done(((bf16[514,1024]{1,0:T(8,128)(2,1)}, bf16[514,1024]{1,0:T(8,128)(2,1)}), (bf16[514,1024]{1,0:T(8,128)(2,1)}, bf16[514,1024]{1,0:T(8,128)(2,1)})) %all-reduce.44.cloned.1.call-update) | async-done | bytes 2105360 | tf_op jit(solution)/shard_map/psum | solution.py:79
  658.8 6.2 fusion.152
  667.3 16.8 %collective-permute-done.5 = bf16[514,1024]{1,0:T(8,128)(2,1)S(1)} collective-permute-done((bf16[514,1024]{1,0:T(8,128)(2,1)S(1)}, bf16[514,1024]{1,0:T(8,128)(2,1)S(1)}, u32[]{:S(2)}, u32[]{:S(2)}) %collective-permute-start.5) | collective-permute-done | bytes 1052704 | tf_op jit(solution)/shard_map/ppermute | solution.py:17
  684.3 7.0 convert_reduce_fusion.16
  694.7 5.6 fusion.474
  700.3 5.1 fusion.482
  705.5 40.7 %all-reduce.42.cloned.1.call-done = (bf16[514,1024]{1,0:T(8,128)(2,1)}, bf16[514,1024]{1,0:T(8,128)(2,1)}) async-done(((bf16[514,1024]{1,0:T(8,128)(2,1)}, bf16[514,1024]{1,0:T(8,128)(2,1)}), (bf16[514,1024]{1,0:T(8,128)(2,1)}, bf16[514,1024]{1,0:T(8,128)(2,1)})) %all-reduce.42.cloned.1.call-update) | async-done | bytes 2105360 | tf_op jit(solution)/shard_map/psum | solution.py:87
  746.1 4.5 broadcast_select_fusion.15
  750.7 4.2 collective-permute-start.3
  763.2 13.5 collective-permute-done.3
  896.6 6.4 all-reduce.40.cloned.1.call-done
  915.1 7.2 fusion.166
  922.3 18.4 %collective-permute-done.6 = bf16[514,1024]{1,0:T(8,128)(2,1)S(1)} collective-permute-done((bf16[514,1024]{1,0:T(8,128)(2,1)S(1)}, bf16[514,1024]{1,0:T(8,128)(2,1)S(1)}, u32[]{:S(2)}, u32[]{:S(2)}) %collective-permute-start.6) | collective-permute-done | bytes 1052704 | tf_op jit(solution)/shard_map/ppermute | solution.py:17
  940.8 6.9 convert_reduce_fusion.15
  954.6 4.0 fusion.386
  958.6 28.3 %all-reduce.30.cloned.1.call-done = bf16[514,1024]{1,0:T(8,128)(2,1)} async-done(((bf16[514,1024]{1,0:T(8,128)(2,1)}), bf16[514,1024]{1,0:T(8,128)(2,1)}) %all-reduce.30.cloned.1.call-update) | async-done | bytes 1052688 | tf_op jit(solution)/shard_map/psum | solution.py:141
  986.9 5.2 fusion.201
  1021.0 4.1 add_convert_fusion.4
  1025.3 7.5 fusion.480
  1032.8 29.3 %all-reduce.32.cloned.1.call-done = bf16[514,1024]{1,0:T(8,128)(2,1)} async-done(((bf16[514,1024]{1,0:T(8,128)(2,1)}), bf16[514,1024]{1,0:T(8,128)(2,1)}) %all-reduce.32.cloned.1.call-update) | async-done | bytes 1052688 | tf_op jit(solution)/shard_map/psum | solution.py:196
  1082.6 14.5 collective-permute-done.7
  1097.3 7.0 convert_reduce_fusion.14
  1107.9 12.2 fusion.326
  1125.4 17.9 %all-reduce.34.cloned.1.call-done = bf16[514,1024]{1,0:T(8,128)(2,1)} async-done(((bf16[514,1024]{1,0:T(8,128)(2,1)}), bf16[514,1024]{1,0:T(8,128)(2,1)}) %all-reduce.34.cloned.1.call-update) | async-done | bytes 1052688 | tf_op jit(solution)/shard_map/psum | solution.py:141
  1143.3 4.9 fusion.209
  1148.3 7.2 fusion.163
  1196.6 3.9 fusion.423
  1201.3 4.5 fusion.358
  1223.7 22.6 %all-reduce.38.cloned.1.call-done = (bf16[514,1024]{1,0:T(8,128)(2,1)}, bf16[514,1024]{1,0:T(8,128)(2,1)}) async-done(((bf16[514,1024]{1,0:T(8,128)(2,1)}, bf16[514,1024]{1,0:T(8,128)(2,1)}), (bf16[514,1024]{1,0:T(8,128)(2,1)}, bf16[514,1024]{1,0:T(8,128)(2,1)})) %all-reduce.38.cloned.1.call-update) | async-done | bytes 2105360 | tf_op jit(solution)/shard_map/psum | solution.py:87
  1246.3 4.2 fusion.470
  1252.9 4.8 pad_maximum_fusion.1
  1257.7 8.7 copy.536
  1273.6 4.0 pad_maximum_fusion
  1277.7 8.2 copy.537
  1289.6 23.3 %all-reduce = (bf16[1,8,1024]{2,1,0:T(8,128)(2,1)S(1)}, bf16[1,2,256]{2,1,0:T(2,128)(2,1)S(1)}, bf16[1,1024]{1,0:T(2,128)(2,1)S(1)}) all-reduce(bf16[1,8,1024]{2,1,0:T(8,128)(2,1)S(1)} %fusion.594, bf16[1,2,256]{2,1,0:T(2,128)(2,1)S(1)} %fusion.600, ...), channel_id=1, replica_groups=mesh['section'=2,'tensor'=4,'dp'=4] {'dp'}, use_global_device_ids=true, to_apply=%region_115.116 | all-reduce | flops 9728 | bytes 38912 | tf_op jit(solution)/shard_map/psum | solution.py:257
  1314.6 159.1 %all-reduce.36.cloned.1.call-done = (bf16[1,3,1024,256]{3,2,1,0:T(8,128)(2,1)}, bf16[1,256,1024]{2,1,0:T(8,128)(2,1)}, bf16[1,1024,1024]{2,1,0:T(8,128)(2,1)}, bf16[1,1024,1024]{2,1,0:T(8,128)(2,1)}) async-done(((bf16[1,3,1024,256]{3,2,1,0:T(8,128)(2,1)}, bf16[1,256,1024]{2,1,0:T(8,128)(2,1)}, bf16[1,1024,1024]{2,1,0:T(8,128)(2,1)}, bf16[1,1024,1024]{2,1,0:T(8,128)(2,1)}), ...) | async-done | bytes 6291472 | tf_op jit(solution)/shard_map/psum | solution.py:258
  (1188 shorter events, 570.2 us)
Async XLA Ops:
  7.2 74.0 %copy-start = (bf16[1,1024,1024]{2,1,0:T(8,128)(2,1)S(1)}, bf16[1,1024,1024]{2,1,0:T(8,128)(2,1)}, u32[]{:S(2)}) copy-start(bf16[1,1024,1024]{2,1,0:T(8,128)(2,1)} %param.15) | copy-start | bytes 6291460
  7.2 71.2 %all-reduce.24.cloned.1.call-start = ((), (), s32[]{:S(2)}) async-start(), calls=%async_computation | async-start | bytes 2129920 | tf_op jit(solution)/shard_map/psum | solution.py:79
  8.3 72.9 %copy-start.304 = (f32[1,1,1024]{2,1,0:T(1,128)}, f32[1,1,1024]{2,1,0:T(1,128)S(1)}, u32[]{:S(2)}) copy-start(f32[1,1,1024]{2,1,0:T(1,128)S(1)} %get-tuple-element.206) | copy-start | bytes 12292
  8.3 737.8 %copy-start.226 = (f32[1,1,1024]{2,1,0:T(1,128)}, f32[1,1,1024]{2,1,0:T(1,128)S(1)}, u32[]{:S(2)}) copy-start(f32[1,1,1024]{2,1,0:T(1,128)S(1)} %get-tuple-element.205) | copy-start | bytes 12292
  22.2 141.1 %copy-start.362 = (f32[1,1,256]{2,1,0:T(1,128)}, f32[1,1,256]{2,1,0:T(1,128)S(1)}, u32[]{:S(2)}) copy-start(f32[1,1,256]{2,1,0:T(1,128)S(1)} %get-tuple-element.224) | copy-start | bytes 3076
  22.2 142.2 %copy-start.358 = (f32[1,1,256]{2,1,0:T(1,128)}, f32[1,1,256]{2,1,0:T(1,128)S(1)}, u32[]{:S(2)}) copy-start(f32[1,1,256]{2,1,0:T(1,128)S(1)} %get-tuple-element.223) | copy-start | bytes 3076
  39.4 89.2 %all-reduce.26.cloned.1.call-start = ((), (), s32[]{:S(2)}) async-start(), calls=%async_computation.1 | async-start | bytes 2129920 | tf_op jit(solution)/shard_map/psum | solution.py:87
  50.7 30.4 %copy-start.346 = (f32[1,1024]{1,0:T(1,128)}, f32[1,1024]{1,0:T(1,128)S(1)}, u32[]{:S(2)}) copy-start(f32[1,1024]{1,0:T(1,128)S(1)} %add.850) | copy-start | bytes 12292
  91.7 126.0 %all-reduce.28.cloned.1.call-start = ((), (), s32[]{:S(2)}) async-start(), calls=%async_computation.2 | async-start | bytes 2129920 | tf_op jit(solution)/shard_map/psum | solution.py:79
  131.8 26.2 %collective-permute-start = (bf16[514,1024]{1,0:T(8,128)(2,1)}, bf16[514,1024]{1,0:T(8,128)(2,1)}, u32[]{:S(2)}, u32[]{:S(2)}) collective-permute-start(bf16[514,1024]{1,0:T(8,128)(2,1)} %fusion.121), channel_id=1, source_target_pairs={{0,16},{1,17},{2,18},{3,19},{4,20},{5,21},{6,22},{7,23},{8,24},{9,... | collective-permute-start | bytes 3158024 | tf_op jit(solution)/shard_map/ppermute | solution.py:17
  136.7 23.5 %copy-start.257 = (f32[514]{0:T(1024)}, f32[514]{0:T(1024)S(1)}, u32[]{:S(2)}) copy-start(f32[514]{0:T(1024)S(1)} %div.195) | copy-start | bytes 6172
  139.4 20.8 %copy-start.14 = (f32[514,1024]{1,0:T(8,128)S(1)}, f32[514,1024]{1,0:T(8,128)}, u32[]{:S(2)}) copy-start(f32[514,1024]{1,0:T(8,128)} %reshape.844) | copy-start | bytes 6316036
  159.7 284.0 %copy-start.5 = (bf16[514,1024]{1,0:T(8,128)(2,1)}, bf16[514,1024]{1,0:T(8,128)(2,1)S(1)}, u32[]{:S(2)}) copy-start(bf16[514,1024]{1,0:T(8,128)(2,1)S(1)} %get-tuple-element.161) | copy-start | bytes 3158020
  159.7 284.0 %copy-start.236 = (f32[514]{0:T(1024)}, f32[514]{0:T(1024)S(1)}, u32[]{:S(2)}) copy-start(f32[514]{0:T(1024)S(1)} %broadcast_multiply_fusion.28) | copy-start | bytes 6172
  160.2 283.5 %copy-start.252 = (f32[514]{0:T(1024)}, f32[514]{0:T(1024)S(1)}, u32[]{:S(2)}) copy-start(f32[514]{0:T(1024)S(1)} %add_rsqrt_fusion.8) | copy-start | bytes 6172
  172.1 178.5 %copy-start.228 = (f32[2,4,257]{2,1,0:T(4,128)}, f32[2,4,257]{2,1,0:T(4,128)S(1)}, u32[]{:S(2)}) copy-start(f32[2,4,257]{2,1,0:T(4,128)S(1)} %get-tuple-element.229) | copy-start | bytes 24676
  179.9 113.3 %all-reduce.50.cloned.1.call-start = ((), (), s32[]{:S(2)}) async-start(), calls=%async_computation.13 | async-start | bytes 4259840 | tf_op jit(solution)/shard_map/psum | solution.py:87
  187.4 32.9 %copy-start.276 = (f32[514]{0:T(1024)S(1)}, f32[514]{0:T(1024)}, u32[]{:S(2)}) copy-start(f32[514]{0:T(1024)} %copy-done.275) | copy-start | bytes 6172
  187.4 32.9 %copy-start.305 = (f32[1,1,1024]{2,1,0:T(1,128)S(1)}, f32[1,1,1024]{2,1,0:T(1,128)}, u32[]{:S(2)}) copy-start(f32[1,1,1024]{2,1,0:T(1,128)} %copy-done.304) | copy-start | bytes 12292
  187.4 32.9 %copy-start.347 = (f32[1,1024]{1,0:T(1,128)S(1)}, f32[1,1024]{1,0:T(1,128)}, u32[]{:S(2)}) copy-start(f32[1,1024]{1,0:T(1,128)} %copy-done.346) | copy-start | bytes 12292
  219.6 82.1 %copy-start.263 = (f32[514]{0:T(1024)}, f32[514]{0:T(1024)S(1)}, u32[]{:S(2)}) copy-start(f32[514]{0:T(1024)S(1)} %broadcast_multiply_fusion.27) | copy-start | bytes 6172
  220.3 81.4 %copy-start.290 = (f32[514]{0:T(1024)}, f32[514]{0:T(1024)S(1)}, u32[]{:S(2)}) copy-start(f32[514]{0:T(1024)S(1)} %get-tuple-element.222) | copy-start | bytes 6172
  240.5 199.6 %all-reduce.48.cloned.1.call-start = ((), (), s32[]{:S(2)}) async-start(), calls=%async_computation.12 | async-start | bytes 4259840 | tf_op jit(solution)/shard_map/psum | solution.py:79
  297.7 26.0 %collective-permute-start.1 = (bf16[514,1024]{1,0:T(8,128)(2,1)}, bf16[514,1024]{1,0:T(8,128)(2,1)}, u32[]{:S(2)}, u32[]{:S(2)}) collective-permute-start(bf16[514,1024]{1,0:T(8,128)(2,1)} %get-tuple-element.140), channel_id=1, source_target_pairs={{0,16},{1,17},{2,18},{3,19},{4,20},{5,21},{6,22},{7,23},{8,24},{9,... | collective-permute-start | bytes 3158024 | tf_op jit(solution)/shard_map/ppermute | solution.py:17
  309.7 16.8 %copy-start.15 = (f32[514,1024]{1,0:T(8,128)S(1)}, f32[514,1024]{1,0:T(8,128)}, u32[]{:S(2)}) copy-start(f32[514,1024]{1,0:T(8,128)} %reshape.844) | copy-start | bytes 6316036
  309.7 16.8 %copy-start.258 = (f32[514]{0:T(1024)S(1)}, f32[514]{0:T(1024)}, u32[]{:S(2)}) copy-start(f32[514]{0:T(1024)} %copy-done.257) | copy-start | bytes 6172
  386.6 151.6 %all-reduce.46.cloned.1.call-start = ((), (), s32[]{:S(2)}) async-start(), calls=%async_computation.11 | async-start | bytes 4259840 | tf_op jit(solution)/shard_map/psum | solution.py:87
  442.4 154.8 %copy-start.261 = (f32[514]{0:T(1024)}, f32[514]{0:T(1024)S(1)}, u32[]{:S(2)}) copy-start(f32[514]{0:T(1024)S(1)} %broadcast_multiply_fusion.25) | copy-start | bytes 6172
  449.1 27.1 %collective-permute-start.4 = (bf16[514,1024]{1,0:T(8,128)(2,1)S(1)}, bf16[514,1024]{1,0:T(8,128)(2,1)S(1)}, u32[]{:S(2)}, u32[]{:S(2)}) collective-permute-start(bf16[514,1024]{1,0:T(8,128)(2,1)S(1)} %get-tuple-element.154), channel_id=1, source_target_pairs={{16,0},{17,1},{18,2},{19,3},{20,4},{21,5},{22,6},{23,7},{24,8},{25... | collective-permute-start | bytes 3158024 | tf_op jit(solution)/shard_map/ppermute | solution.py:17
  456.8 19.5 %copy-start.386 = (f32[514,1024]{1,0:T(8,128)}, f32[514,1024]{1,0:T(8,128)S(1)}, u32[]{:S(2)}) copy-start(f32[514,1024]{1,0:T(8,128)S(1)} %get-tuple-element.241) | copy-start | bytes 6316036
  456.9 19.3 %copy-start.115 = (bf16[514,1024]{1,0:T(8,128)(2,1)S(1)}, bf16[514,1024]{1,0:T(8,128)(2,1)}, u32[]{:S(2)}) copy-start(bf16[514,1024]{1,0:T(8,128)(2,1)} %reshape_squeeze.25) | copy-start | bytes 3158020
  459.1 17.2 %copy-start.385 = (f32[514,1024]{1,0:T(8,128)S(1)}, f32[514,1024]{1,0:T(8,128)}, u32[]{:S(2)}) copy-start(f32[514,1024]{1,0:T(8,128)} %get-tuple-element.228) | copy-start | bytes 6316036
  486.7 161.9 %all-reduce.44.cloned.1.call-start = ((), (), s32[]{:S(2)}) async-start(), calls=%async_computation.10 | async-start | bytes 4259840 | tf_op jit(solution)/shard_map/psum | solution.py:79
  508.8 29.5 %copy-start.11 = (bf16[514,1024]{1,0:T(8,128)(2,1)S(1)}, bf16[514,1024]{1,0:T(8,128)(2,1)}, u32[]{:S(2)}) copy-start(bf16[514,1024]{1,0:T(8,128)(2,1)} %copy-done.9) | copy-start | bytes 3158020
  542.8 31.1 %collective-permute-start.2 = (bf16[514,1024]{1,0:T(8,128)(2,1)}, bf16[514,1024]{1,0:T(8,128)(2,1)}, u32[]{:S(2)}, u32[]{:S(2)}) collective-permute-start(bf16[514,1024]{1,0:T(8,128)(2,1)} %get-tuple-element.142), channel_id=1, source_target_pairs={{0,16},{1,17},{2,18},{3,19},{4,20},{5,21},{6,22},{7,23},{8,24},{9,... | collective-permute-start | bytes 3158024 | tf_op jit(solution)/shard_map/ppermute | solution.py:17
  597.1 149.0 %all-reduce.42.cloned.1.call-start = ((), (), s32[]{:S(2)}) async-start(), calls=%async_computation.9 | async-start | bytes 4259840 | tf_op jit(solution)/shard_map/psum | solution.py:87
  650.5 104.4 %copy-start.250 = (f32[514]{0:T(1024)}, f32[514]{0:T(1024)S(1)}, u32[]{:S(2)}) copy-start(f32[514]{0:T(1024)S(1)} %broadcast_multiply_fusion.23) | copy-start | bytes 6172
  651.2 103.7 %copy-start.270 = (f32[514]{0:T(1024)}, f32[514]{0:T(1024)S(1)}, u32[]{:S(2)}) copy-start(f32[514]{0:T(1024)S(1)} %get-tuple-element.215) | copy-start | bytes 6172
  657.0 27.1 %collective-permute-start.5 = (bf16[514,1024]{1,0:T(8,128)(2,1)S(1)}, bf16[514,1024]{1,0:T(8,128)(2,1)S(1)}, u32[]{:S(2)}, u32[]{:S(2)}) collective-permute-start(bf16[514,1024]{1,0:T(8,128)(2,1)S(1)} %convert_element_type.956), channel_id=1, source_target_pairs={{16,0},{17,1},{18,2},{19,3},{20,4},{21,5},{22,6},{23,7},{24,8},{25... | collective-permute-start | bytes 3158024 | tf_op jit(solution)/shard_map/ppermute | solution.py:17
  665.0 19.2 %copy-start.390 = (f32[514,1024]{1,0:T(8,128)}, f32[514,1024]{1,0:T(8,128)S(1)}, u32[]{:S(2)}) copy-start(f32[514,1024]{1,0:T(8,128)S(1)} %get-tuple-element.247) | copy-start | bytes 6316036
  665.0 19.1 %copy-start.114 = (bf16[514,1024]{1,0:T(8,128)(2,1)S(1)}, bf16[514,1024]{1,0:T(8,128)(2,1)}, u32[]{:S(2)}) copy-start(bf16[514,1024]{1,0:T(8,128)(2,1)} %reshape_squeeze.26) | copy-start | bytes 3158020
  667.3 16.9 %copy-start.389 = (f32[514,1024]{1,0:T(8,128)S(1)}, f32[514,1024]{1,0:T(8,128)}, u32[]{:S(2)}) copy-start(f32[514,1024]{1,0:T(8,128)} %copy-done.388) | copy-start | bytes 6316036
  694.6 208.5 %all-reduce.40.cloned.1.call-start = ((), (), s32[]{:S(2)}) async-start(), calls=%async_computation.8 | async-start | bytes 4259840 | tf_op jit(solution)/shard_map/psum | solution.py:79
  750.7 26.0 %collective-permute-start.3 = (bf16[514,1024]{1,0:T(8,128)(2,1)}, bf16[514,1024]{1,0:T(8,128)(2,1)}, u32[]{:S(2)}, u32[]{:S(2)}) collective-permute-start(bf16[514,1024]{1,0:T(8,128)(2,1)} %get-tuple-element.144), channel_id=1, source_target_pairs={{0,16},{1,17},{2,18},{3,19},{4,20},{5,21},{6,22},{7,23},{8,24},{9,... | collective-permute-start | bytes 3158024 | tf_op jit(solution)/shard_map/ppermute | solution.py:17
  849.5 137.3 %all-reduce.30.cloned.1.call-start = ((), (), s32[]{:S(2)}) async-start(), calls=%async_computation.3 | async-start | bytes 2129920 | tf_op jit(solution)/shard_map/psum | solution.py:141
  913.6 27.1 %collective-permute-start.6 = (bf16[514,1024]{1,0:T(8,128)(2,1)S(1)}, bf16[514,1024]{1,0:T(8,128)(2,1)S(1)}, u32[]{:S(2)}, u32[]{:S(2)}) collective-permute-start(bf16[514,1024]{1,0:T(8,128)(2,1)S(1)} %convert_element_type.974), channel_id=1, source_target_pairs={{16,0},{17,1},{18,2},{19,3},{20,4},{21,5},{22,6},{23,7},{24,8},{25... | collective-permute-start | bytes 3158024 | tf_op jit(solution)/shard_map/ppermute | solution.py:17
  915.1 25.6 %copy-start.86 = (bf16[514,1024]{1,0:T(8,128)(2,1)S(1)}, bf16[514,1024]{1,0:T(8,128)(2,1)}, u32[]{:S(2)}) copy-start(bf16[514,1024]{1,0:T(8,128)(2,1)} %reshape_squeeze.27) | copy-start | bytes 3158020
  915.1 25.7 %copy-start.387 = (f32[514,1024]{1,0:T(8,128)S(1)}, f32[514,1024]{1,0:T(8,128)}, u32[]{:S(2)}) copy-start(f32[514,1024]{1,0:T(8,128)} %copy-done.386) | copy-start | bytes 6316036
  922.3 25.5 %copy-start.392 = (f32[514,1024]{1,0:T(8,128)}, f32[514,1024]{1,0:T(8,128)S(1)}, u32[]{:S(2)}) copy-start(f32[514,1024]{1,0:T(8,128)S(1)} %get-tuple-element.256) | copy-start | bytes 6316036
  922.3 18.5 %copy-start.370 = (bf16[1,1024,1024]{2,1,0:T(8,128)(2,1)S(1)}, bf16[1,1024,1024]{2,1,0:T(8,128)(2,1)}, u32[]{:S(2)}) copy-start(bf16[1,1024,1024]{2,1,0:T(8,128)(2,1)} %param.17) | copy-start | bytes 6291460
  951.1 111.0 %all-reduce.32.cloned.1.call-start = ((), (), s32[]{:S(2)}) async-start(), calls=%async_computation.4 | async-start | bytes 2129920 | tf_op jit(solution)/shard_map/psum | solution.py:196
  954.6 32.3 %copy-start.262 = (f32[514]{0:T(1024)S(1)}, f32[514]{0:T(1024)}, u32[]{:S(2)}) copy-start(f32[514]{0:T(1024)} %copy-done.261) | copy-start | bytes 6172
  954.6 32.3 %copy-start.289 = (f32[514]{0:T(1024)S(1)}, f32[514]{0:T(1024)}, u32[]{:S(2)}) copy-start(f32[514]{0:T(1024)} %copy-done.286) | copy-start | bytes 6172
  958.6 33.5 %copy-start.328 = (f32[514]{0:T(1024)S(1)}, f32[514]{0:T(1024)}, u32[]{:S(2)}) copy-start(f32[514]{0:T(1024)} %get-tuple-element.213) | copy-start | bytes 6172
  1025.2 36.9 %copy-start.240 = (f32[514]{0:T(1024)S(1)}, f32[514]{0:T(1024)}, u32[]{:S(2)}) copy-start(f32[514]{0:T(1024)} %copy-done.238) | copy-start | bytes 6172
  1025.2 36.9 %copy-start.256 = (f32[514]{0:T(1024)S(1)}, f32[514]{0:T(1024)}, u32[]{:S(2)}) copy-start(f32[514]{0:T(1024)} %copy-done.254) | copy-start | bytes 6172
  1025.2 118.1 %all-reduce.34.cloned.1.call-start = ((), (), s32[]{:S(2)}) async-start(), calls=%async_computation.5 | async-start | bytes 2129920 | tf_op jit(solution)/shard_map/psum | solution.py:141
  1032.8 32.8 %copy-start.330 = (f32[514]{0:T(1024)S(1)}, f32[514]{0:T(1024)}, u32[]{:S(2)}) copy-start(f32[514]{0:T(1024)} %get-tuple-element.210) | copy-start | bytes 6172
  1069.5 27.5 %collective-permute-start.7 = (bf16[514,1024]{1,0:T(8,128)(2,1)S(1)}, bf16[514,1024]{1,0:T(8,128)(2,1)S(1)}, u32[]{:S(2)}, u32[]{:S(2)}) collective-permute-start(bf16[514,1024]{1,0:T(8,128)(2,1)S(1)} %convert_element_type.992), channel_id=1, source_target_pairs={{16,0},{17,1},{18,2},{19,3},{20,4},{21,5},{22,6},{23,7},{24,8},{25... | collective-permute-start | bytes 3158024 | tf_op jit(solution)/shard_map/ppermute | solution.py:17
  1079.2 18.0 %copy-start.393 = (f32[514,1024]{1,0:T(8,128)S(1)}, f32[514,1024]{1,0:T(8,128)}, u32[]{:S(2)}) copy-start(f32[514,1024]{1,0:T(8,128)} %copy-done.392) | copy-start | bytes 6316036
  1107.6 138.7 %all-reduce.38.cloned.1.call-start = ((), (), s32[]{:S(2)}) async-start(), calls=%async_computation.7 | async-start | bytes 4259840 | tf_op jit(solution)/shard_map/psum | solution.py:87
  1125.4 22.8 %copy-start.326 = (f32[514]{0:T(1024)S(1)}, f32[514]{0:T(1024)}, u32[]{:S(2)}) copy-start(f32[514]{0:T(1024)} %get-tuple-element.211) | copy-start | bytes 6172
  1193.6 280.2 %all-reduce.36.cloned.1.call-start = ((), (), s32[]{:S(2)}) async-start(), calls=%async_computation.6 | async-start | bytes 12582912 | tf_op jit(solution)/shard_map/psum | solution.py:258
  1220.3 26.0 %copy-start.227 = (f32[1,1,1024]{2,1,0:T(1,128)S(1)}, f32[1,1,1024]{2,1,0:T(1,128)}, u32[]{:S(2)}) copy-start(f32[1,1,1024]{2,1,0:T(1,128)} %copy-done.226) | copy-start | bytes 12292
  (352 other events, 1474.7 us)
Sparse Core Ops, SparseCore 0:
  39.5 38.8 all-reduce.23
  91.8 36.7 all-reduce.25
  180.0 37.7 all-reduce.27
  240.6 52.5 all-reduce.49
  386.8 53.3 all-reduce.47
  486.8 51.4 all-reduce.45
  597.2 51.2 all-reduce.43
  694.7 51.4 all-reduce.41
  849.7 53.3 all-reduce.39
  951.2 35.5 all-reduce.29
  1025.3 36.7 all-reduce.31
  1107.7 35.6 all-reduce.33
  1193.7 52.5 all-reduce.37
  1248.8 224.9 all-reduce.35
where the time goes:
time: 1500 us; the launch traced here: 1490 us
  waiting for transfers between devices  637 us (42%)
  matrix products  340 us (23%)
  local copies, waits for them, and re-layouts  273 us (18%)
  other arithmetic  171 us (11%)
  starting transfers between devices  26.2 us (2%)
  blocking collectives  23.3 us (2%)
  between operations  18.5 us (1%)
    psum x5, waiting for transfers between devices, layer_forward(): lax.psum(matmul(hidden_low, fc2_weight).astype(jnp.bfloat16), 'tensor')  164 us
    psum x1, waiting for transfers between devices, body(): lax.psum(sums[1].astype(jnp.bfloat16), 'dp').astype(jnp.float32)  159 us
    psum x5, waiting for transfers between devices, layer_forward(): lax.psum(matmul(mixed_low, out_weight).astype(jnp.bfloat16), 'tensor')  126 us
    ppermute x8, waiting for transfers between devices, passed_along(): return lax.ppermute(block, axis, route)  113 us
    dot_general x30, matrix products, matmul_left(): lax.dot_general(left, right, (((0,), (0,)), ((), ())), preferred_element_...  107 us
    dot_general x30, matrix products, matmul_right(): lax.dot_general(left, right, (((1,), (1,)), ((), ())), preferred_element_...  90.9 us
    dot_general x30, matrix products, matmul(): return jnp.dot(left, right, preferred_element_type=jnp.float32)  80.4 us
    psum x2, waiting for transfers between devices, layer_backward(): lax.psum(matmul_right(grad_pre, fc1_weight).astype(jnp.bfloat16), 'tensor')  46.2 us
  transfers between devices with their start and end apart: 22, of which 21 were waited for; matrix products, arithmetic and copies ran while one was open for 23% of the time, Pallas kernels for 0%

commit v1 on v0

v1 whole, which is shorter than its diff:
```python
from functools import partial

import jax
import jax.numpy as jnp
from jax import lax
from jax.experimental import pallas as pl
from jax.experimental.pallas import tpu as pltpu
from jax.sharding import PartitionSpec as P

HD = 64
LAG = 2
EPS = 1e-06
LOW = jnp.bfloat16
F32 = jnp.float32
VMEM_BYTES = 40 * 1024 * 1024


def dot_nn(a, b):
    return jnp.dot(a, b, preferred_element_type=F32)


def dot_tn(a, b):
    return lax.dot_general(a, b, (((0,), (0,)), ((), ())), preferred_element_type=F32)


def dot_nt(a, b):
    return lax.dot_general(a, b, (((1,), (1,)), ((), ())), preferred_element_type=F32)


def unit_rows_of(x):
    center = x - jnp.mean(x, axis=-1, keepdims=True)
    inverse = lax.rsqrt(jnp.mean(center * center, axis=-1, keepdims=True) + EPS)
    return center * inverse, inverse


def norm_back(upstream, unit, inverse, gain):
    scaled = upstream * gain
    inner = jnp.mean(scaled * unit, axis=-1, keepdims=True)
    return inverse * (scaled - jnp.mean(scaled, axis=-1, keepdims=True) - unit * inner)


def col_sum(x):
    return jnp.sum(x, axis=0, keepdims=True)


def split_out(flags, part, mine_ref, send_ref):
    half = part.shape[1] // 2
    low_core = flags[1] == 0
    lo, hi = part[:, :half], part[:, half:]
    mine_ref[...] = jnp.where(low_core, lo, hi).astype(LOW)
    send_ref[...] = jnp.where(low_core, hi, lo).astype(LOW)


def join(flags, mine_ref, other_ref):
    low_core = flags[1] == 0
    mine, other = mine_ref[...].astype(F32), other_ref[...].astype(F32)
    return jnp.concatenate(
        [jnp.where(low_core, mine, other), jnp.where(low_core, other, mine)], axis=1
    )


def probs_of(q, k, seq):
    s = dot_nt(q, k) * HD ** (-0.5)
    cols = lax.broadcasted_iota(jnp.int32, s.shape, 1)
    s = jnp.where(cols < seq, s, -1e30)
    e = jnp.exp(s - jnp.max(s, axis=-1, keepdims=True))
    return e * (1.0 / jnp.sum(e, axis=-1, keepdims=True))


def attn_fwd_kernel(seq, flags, own, arrived, vec, wqkv, qvb, wout, x_o, n1_o, qkv_o, o_o, mine_o, send_o):
    x16 = jnp.where(flags[0] == 1, own[0].astype(F32), arrived[0].astype(F32))
    x_o[...] = x16.astype(LOW)
    unit, _ = unit_rows_of(x16)
    n1 = (unit * vec[0:1, :] + vec[1:2, :]).astype(LOW)
    n1_o[...] = n1
    share = wqkv.shape[2]
    q = (dot_nn(n1, wqkv[0]) + qvb[0:1, :]).astype(LOW)
    k = dot_nn(n1, wqkv[1]).astype(LOW)
    v = (dot_nn(n1, wqkv[2]) + qvb[1:2, :]).astype(LOW)
    qkv_o[:, 0:share] = q
    qkv_o[:, share : 2 * share] = k
    qkv_o[:, 2 * share :] = v
    heads = []
    for h in range(share // HD):
        cut = slice(h * HD, (h + 1) * HD)
        p = probs_of(q[:, cut], k[:, cut], seq).astype(LOW)
        heads.append(dot_nn(p, v[:, cut]))
    o = jnp.concatenate(heads, axis=1).astype(LOW)
    o_o[...] = o
    split_out(flags, dot_nn(o, wout[...]), mine_o, send_o)


def mlp_fwd_kernel(flags, x, a_m, a_s, vec, fc1, fc1b, fc2, n2_o, g_o, dg_o, mine_o, send_o):
    a = join(flags, a_m, a_s)
    h1 = x[...].astype(F32) + vec[3:4, :] * (a + vec[2:3, :])
    unit, _ = unit_rows_of(h1)
    n2 = (unit * vec[4:5, :] + vec[5:6, :]).astype(LOW)
    n2_o[...] = n2
    width = fc1.shape[1]
    chunk = min(width, 256)
    total = None
    for c in range(0, width, chunk):
        cut = slice(c, c + chunk)
        u = dot_nn(n2, fc1[:, cut]) + fc1b[:, cut]
        phi = 0.5 * (1.0 + lax.erf(u * (2.0 ** -0.5)))
        g = (u * phi).astype(LOW)
        g_o[:, cut] = g
        dens = jnp.exp(-0.5 * u * u) * 0.3989422804014327
        dg_o[:, cut] = (phi + u * dens).astype(LOW)
        term = dot_nn(g, fc2[cut, :])
        total = term if total is None else total + term
    split_out(flags, total, mine_o, send_o)


def out_kernel(flags, x, a_m, a_s, m_m, m_s, vec, y_o):
    h1 = x[...].astype(F32) + vec[3:4, :] * (join(flags, a_m, a_s) + vec[2:3, :])
    y_o[0] = (h1 + vec[7:8, :] * (join(flags, m_m, m_s) + vec[6:7, :])).astype(LOW)


def mlp_bwd_kernel(flags, cot, returned, m_m, m_s, dg, vec, fc1, fc2, dy_o, dm_o, du_o, mine_o, send_o, sums_o):
    dy = jnp.where(flags[0] == 1, returned[0].astype(F32), cot[0].astype(F32))
    dy_o[...] = dy.astype(LOW)
    m = join(flags, m_m, m_s)
    scaled = dy * vec[7:8, :]
    sums_o[0:1, :] = col_sum(scaled)
    sums_o[1:2, :] = col_sum(dy * (m + vec[6:7, :]))
    dm = scaled.astype(LOW)
    dm_o[...] = dm
    width = fc1.shape[1]
    chunk = min(width, 256)
    total = None
    for c in range(0, width, chunk):
        cut = slice(c, c + chunk)
        du = (dot_nt(dm, fc2[cut, :]) * dg[:, cut].astype(F32)).astype(LOW)
        du_o[:, cut] = du
        sums_o[2:3, cut] = col_sum(du.astype(F32))
        term = dot_nt(du, fc1[:, cut])
        total = term if total is None else total + term
    split_out(flags, total, mine_o, send_o)


def attn_bwd_kernel(
    seq, flags, x, a_m, a_s, dy, d_m, d_s, qkv, vec, wqkv, wout, dh_o, da_o, dqkv_o, mine_o, send_o, sums_o, pair_o
):
    a = join(flags, a_m, a_s) + vec[2:3, :]
    h1 = x[...].astype(F32) + vec[3:4, :] * a
    unit, inverse = unit_rows_of(h1)
    dn2 = join(flags, d_m, d_s)
    sums_o[0:1, :] = col_sum(dn2 * unit)
    sums_o[1:2, :] = col_sum(dn2)
    dh1 = dy[...].astype(F32) + norm_back(dn2, unit, inverse, vec[4:5, :])
    dh_o[...] = dh1
    scaled = dh1 * vec[3:4, :]
    sums_o[2:3, :] = col_sum(scaled)
    sums_o[3:4, :] = col_sum(dh1 * a)
    da = scaled.astype(LOW)
    da_o[...] = da
    do = dot_nt(da, wout[...]).astype(LOW)
    share = wqkv.shape[2]
    dqs, dks, dvs = [], [], []
    for h in range(share // HD):
        cut = slice(h * HD, (h + 1) * HD)
        q = qkv[:, h * HD : (h + 1) * HD]
        k = qkv[:, share + h * HD : share + (h + 1) * HD]
        v = qkv[:, 2 * share + h * HD : 2 * share + (h + 1) * HD]
        p = probs_of(q, k, seq)
        dvs.append(dot_tn(p.astype(LOW), do[:, cut]))
        dp = dot_nt(do[:, cut], v)
        ds = (p * (dp - jnp.sum(p * dp, axis=-1, keepdims=True))).astype(LOW)
        dqs.append(dot_nn(ds, k) * HD ** (-0.5))
        dks.append(dot_tn(ds, q) * HD ** (-0.5))
    dq = jnp.concatenate(dqs, axis=1).astype(LOW)
    dk = jnp.concatenate(dks, axis=1).astype(LOW)
    dv = jnp.concatenate(dvs, axis=1).astype(LOW)
    dqkv_o[:, 0:share] = dq
    dqkv_o[:, share : 2 * share] = dk
    dqkv_o[:, 2 * share :] = dv
    pair_o[0:1, :] = col_sum(dq.astype(F32))
    pair_o[1:2, :] = col_sum(dv.astype(F32))
    split_out(flags, dot_nt(dq, wqkv[0]) + dot_nt(dk, wqkv[1]) + dot_nt(dv, wqkv[2]), mine_o, send_o)


def in_bwd_kernel(flags, x, dh, d_m, d_s, vec, dx_o, low_o, sums_o):
    unit, inverse = unit_rows_of(x[...].astype(F32))
    dn1 = join(flags, d_m, d_s)
    sums_o[0:1, :] = col_sum(dn1 * unit)
    sums_o[1:2, :] = col_sum(dn1)
    dx = dh[...] + norm_back(dn1, unit, inverse, vec[0:1, :])
    dx_o[...] = dx[: dx_o.shape[0]]
    low_o[0] = dx.astype(LOW)


def weight_kernel(count, *refs):
    lefts, rights, out = refs[:count], refs[count : 2 * count], refs[2 * count]
    total = dot_tn(lefts[0][...], rights[0][...])
    for n in range(1, count):
        total = total + dot_tn(lefts[n][...], rights[n][...])
    out[0] = total.astype(out.dtype)


def whole(shape, block=None, pick=None):
    block = shape if block is None else block
    at = (0,) * len(shape) if pick is None else pick
    return pl.BlockSpec(block, lambda i: at)


def call(kernel, args, outs, picks=None, flops=0):
    picks = picks or {}
    specs = [pl.BlockSpec(memory_space=pltpu.SMEM)]
    for n, arg in enumerate(args[1:], 1):
        if n in picks:
            specs.append(whole(arg.shape, (1,) + arg.shape[1:], (picks[n], 0, 0)))
        else:
            specs.append(whole(arg.shape))
    moved = sum(a.size * a.dtype.itemsize for a in args[1:])
    return pl.pallas_call(
        kernel,
        grid=(1,),
        in_specs=specs,
        out_specs=[whole(s.shape) for s in outs],
        out_shape=outs,
        compiler_params=pltpu.CompilerParams(vmem_limit_bytes=VMEM_BYTES),
        cost_estimate=pl.CostEstimate(flops=flops, bytes_accessed=moved, transcendentals=0),
    )(*args)


def weight_grad(lefts, rights, blocks):
    count = len(lefts)
    rows, depth = lefts[0].shape
    width = rights[0].shape[1]
    block = width // blocks
    return pl.pallas_call(
        partial(weight_kernel, count),
        grid=(blocks,),
        in_specs=[pl.BlockSpec((rows, depth), lambda i: (0, 0))] * count
        + [pl.BlockSpec((rows, block), lambda i: (0, i))] * count,
        out_specs=pl.BlockSpec((1, depth, block), lambda i: (i, 0, 0)),
        out_shape=jax.ShapeDtypeStruct((blocks, depth, block), LOW),
        compiler_params=pltpu.CompilerParams(vmem_limit_bytes=VMEM_BYTES),
        cost_estimate=pl.CostEstimate(
            flops=2 * count * rows * depth * width,
            bytes_accessed=2 * count * rows * (depth + width) + 2 * depth * width,
            transcendentals=0,
        ),
    )(*lefts, *rights)


def swap(value, bit):
    route = [(i, i ^ bit) for i in range(lax.axis_size("tensor"))]
    return lax.ppermute(value, "tensor", route)


def tensor_sum(mine, send):
    size = lax.axis_size("tensor")
    got = swap(send, 1)
    held = (mine.astype(F32) + got.astype(F32)).astype(LOW)
    bit = 2
    while bit < size:
        got = swap(held, bit)
        held = (held.astype(F32) + got.astype(F32)).astype(LOW)
        bit *= 2
    return held, swap(held, 1)


def passed_along(block, distance):
    devices = range(lax.axis_size("section"))
    route = [(i - distance, i) for i in devices if i - distance in devices]
    return lax.ppermute(block, "section", route)


def body(tokens, cotangent, vectors, w_qkv, qv_bias, w_out, w_fc1, fc1_bias, w_fc2):
    micro_count, images, seq, width = tokens.shape
    units = micro_count * images
    rows = -(-seq // 16) * 16
    wqkv, wout, fc1, fc2 = w_qkv[0], w_out[0], w_fc1[0], w_fc2[0]
    share, hidden = wqkv.shape[2], fc1.shape[1]
    vec = vectors[0].astype(F32)
    qvb = qv_bias[0].astype(F32)
    fc1b = fc1_bias.astype(F32)
    first = lax.axis_index("section") == 0
    flags = jnp.stack([first.astype(jnp.int32), (lax.axis_index("tensor") % 2).astype(jnp.int32)])
    pad = ((0, 0), (0, rows - seq), (0, 0))
    own = jnp.pad(tokens.reshape(units, seq, width), pad)
    cot = jnp.pad(cotangent.reshape(units, seq, width), pad)
    zeros = jnp.zeros((1, rows, width), LOW)

    def low(*shape):
        return jax.ShapeDtypeStruct(shape, LOW)

    def wide(*shape):
        return jax.ShapeDtypeStruct(shape, F32)

    halves = [low(rows, width // 2)] * 2
    ticks = units + LAG
    unit_flops = 2 * rows * width
    arrivals, results, records = {}, [], []
    for t in range(ticks):
        x, n1, qkv, o, mine, send = call(
            partial(attn_fwd_kernel, seq),
            (flags, own if t < units else zeros, arrivals.get(t, zeros), vec, wqkv, qvb, wout),
            [low(rows, width), low(rows, width), low(rows, 3 * share), low(rows, share)] + halves,
            {1: t} if t < units else None,
            unit_flops * share * 8,
        )
        a_m, a_s = tensor_sum(mine, send)
        n2, g, dg, mine, send = call(
            mlp_fwd_kernel,
            (flags, x, a_m, a_s, vec, fc1, fc1b, fc2),
            [low(rows, width), low(rows, hidden), low(rows, hidden)] + halves,
            flops=unit_flops * hidden * 3,
        )
        m_m, m_s = tensor_sum(mine, send)
        (y,) = call(out_kernel, (flags, x, a_m, a_s, m_m, m_s, vec), [low(1, rows, width)])
        results.append(y)
        if t + LAG < ticks:
            arrivals[t + LAG] = passed_along(y, 1)
        records.append((x, n1, qkv, o, a_m, a_s, n2, g, dg, m_m, m_s))

    returns, grads, small = {}, [], []
    pieces = [[] for _ in range(4)]
    for t in range(ticks):
        x, n1, qkv, o, a_m, a_s, n2, g, dg, m_m, m_s = records[ticks - 1 - t]
        dy, dm, du, mine, send, sums_mlp = call(
            mlp_bwd_kernel,
            (flags, cot if t < units else zeros, returns.get(t, zeros), m_m, m_s, dg, vec, fc1, fc2),
            [low(rows, width), low(rows, width), low(rows, hidden)] + halves + [wide(3, width)],
            {1: units - 1 - t} if t < units else None,
            unit_flops * hidden * 2,
        )
        d_m, d_s = tensor_sum(mine, send)
        dh, da, dqkv, mine, send, sums_attn, pair = call(
            partial(attn_bwd_kernel, seq),
            (flags, x, a_m, a_s, dy, d_m, d_s, qkv, vec, wqkv, wout),
            [wide(rows, width), low(rows, width), low(rows, 3 * share)] + halves + [wide(4, width), wide(2, share)],
            flops=unit_flops * share * 10,
        )
        d_m, d_s = tensor_sum(mine, send)
        dx, dx_low, sums_in = call(
            in_bwd_kernel,
            (flags, x, dh, d_m, d_s, vec),
            [wide(seq, width), low(1, rows, width), wide(2, width)],
        )
        grads.append(dx)
        if t + LAG < ticks:
            returns[t + LAG] = passed_along(dx_low, -1)
        small.append((sums_mlp, sums_attn, sums_in, pair))
        for piece, pairing in zip(pieces, ((g, dm), (n2, du), (o, da), (n1, dqkv))):
            piece.append(pairing)

    blocks = (2, 2, 2, 3)
    grad_fc2, grad_fc1, grad_out, grad_qkv = [
        weight_grad([p[0] for p in piece], [p[1] for p in piece], n)
        for piece, n in zip(pieces, blocks)
    ]
    sums_mlp, sums_attn, sums_in, pair = [sum(s[1:], s[0]) for s in zip(*small)]
    grad_vec = jnp.concatenate([sums_in, sums_attn[2:4], sums_attn[0:2], sums_mlp[0:2]], axis=0)
    summed = lax.psum(
        (
            grad_fc2,
            grad_fc1,
            grad_qkv,
            grad_out,
            grad_vec.astype(LOW),
            sums_mlp[2:3].astype(LOW),
            pair.astype(LOW),
        ),
        "dp",
    )
    grad_fc2, grad_fc1, grad_qkv, grad_out, grad_vec, grad_fc1b, grad_pair = [
        s.astype(F32) for s in summed
    ]

    def columns(blocked):
        return jnp.concatenate([blocked[n] for n in range(blocked.shape[0])], axis=1)

    shape_out = (1, micro_count, images, seq, width)
    outputs = jnp.stack(
        [jnp.where(first, results[m][0, :seq], results[m + LAG][0, :seq]) for m in range(units)]
    ).reshape(shape_out)
    input_grads = jnp.stack(
        [jnp.where(first, grads[ticks - 1 - m], grads[units - 1 - m]) for m in range(units)]
    ).reshape(shape_out)
    return (
        outputs,
        input_grads,
        grad_vec[None],
        grad_qkv[None],
        grad_pair[None],
        columns(grad_out)[None],
        columns(grad_fc1)[None],
        grad_fc1b,
        columns(grad_fc2)[None],
    )


def solution(mesh):
    return jax.shard_map(
        body,
        mesh=mesh,
        in_specs=(
            P(None, "dp", None, None),
            P(None, "dp", None, None),
            P("section", None, None),
            P("section", None, None, "tensor"),
            P("section", None, "tensor"),
            P("section", "tensor", None),
            P("section", None, "tensor"),
            P("section", "tensor"),
            P("section", "tensor", None),
        ),
        out_specs=(
            P("section", None, "dp", None, None),
            P("section", None, "dp", None, None),
            P("section", None, None),
            P("section", None, None, "tensor"),
            P("section", None, "tensor"),
            P("section", "tensor", None),
            P("section", None, "tensor"),
            P("section", "tensor"),
            P("section", "tensor", None),
        ),
        check_vma=False,
    )
```

time: 1500 us -> 1030 us (0.69)
  matrix products: 340 us -> 0 us
  Pallas kernels: 0 us -> 213 us
  local copies, waits for them, and re-layouts: 273 us -> 105 us
  other arithmetic: 171 us -> 33.7 us
  waiting for transfers between devices: 637 us -> 519 us
  starting transfers between devices: 26.2 us -> 105 us
    psum x14 -> x1, waiting for transfers between devices: 524 us -> 146 us  [body(): lax.psum((grad_fc2, grad_fc1, grad_qkv, grad_out, grad_vec.astype(LOW), s...]
    dot_general x125 -> x0, matrix products: 340 us -> none  [the longest x30 107 us: matmul_left(): lax.dot_general(left, right, (((0,), (0,)), ((), ())), preferred_element_...]
    ppermute x8 -> x136, waiting for transfers between devices: 113 us -> 373 us  [the longest x120 224 us: swap(): return lax.ppermute(value, 'tensor', route)]
    pallas_call x0 -> x64, Pallas kernels: none -> 213 us  [the longest x60 176 us: call(): pl.pallas_call(kernel, grid=(1,), in_specs=specs, out_specs=[whole(s.shap...]
    reshape x65 -> x0, local copies, waits for them, and re-layouts: 109 us -> none  [the longest x10 20.1 us: layer_backward(): key_heads = key_rows.reshape(head_shape)]
    ppermute x8 -> x136, starting transfers between devices: 23.3 us -> 105 us  [the longest x120 71.6 us: swap(): return lax.ppermute(value, 'tensor', route)]
    reduce_sum x38 -> x0, other arithmetic: 76.1 us -> none  [the longest x10 32.2 us: norm_backward(): jnp.sum(upstream * unit_rows, axis=0)]
    unnamed x792 -> x794, local copies, waits for them, and re-layouts: 45.7 us -> 100 us
  transfers between devices with their start and end apart: 22 -> 137, of which waited for: 21 -> 55; matrix products, arithmetic and copies ran while one was open for 23% -> 4% of each run, Pallas kernels for 0% -> 19%
where the time goes in v1:
time: 1030 us; the launch traced here: 1020 us
  waiting for transfers between devices  519 us (50%)
  Pallas kernels  213 us (21%)
  starting transfers between devices  105 us (10%)
  local copies, waits for them, and re-layouts  105 us (10%)
  other arithmetic  33.7 us (3%)
  blocking collectives  21.3 us (2%)
  between operations  20.2 us (2%)
    ppermute x120, waiting for transfers between devices, swap(): return lax.ppermute(value, 'tensor', route)  224 us
    pallas_call x60, Pallas kernels, call(): pl.pallas_call(kernel, grid=(1,), in_specs=specs, out_specs=[whole(s.shap...  176 us
    ppermute x16, waiting for transfers between devices, passed_along(): return lax.ppermute(block, 'section', route)  149 us
    psum x1, waiting for transfers between devices, body(): lax.psum((grad_fc2, grad_fc1, grad_qkv, grad_out, grad_vec.astype(LOW), s...  146 us
    unnamed x794, local copies, waits for them, and re-layouts  100 us
    ppermute x120, starting transfers between devices, swap(): return lax.ppermute(value, 'tensor', route)  71.6 us
    pallas_call x4, Pallas kernels, weight_grad(): pl.pallas_call(partial(weight_kernel, count), grid=(blocks,), in_specs=[p...  37.5 us
    ppermute x16, starting transfers between devices, passed_along(): return lax.ppermute(block, 'section', route)  33.3 us
  transfers between devices with their start and end apart: 137, of which 55 were waited for; matrix products, arithmetic and copies ran while one was open for 4% of the time, Pallas kernels for 19%

profile of v1, /device:TPU:0, one launch (start us, length us, event | category | flops | bytes accessed | tf_op | source)
XLA Modules:
  0.0 1017.3 jit_solution(10412257794144906212)
XLA Ops:
  8.6 5.6 copy.18
  29.6 6.2 collective-permute-done.14
  53.4 6.2 collective-permute-done.17
  72.4 10.5 %collective-permute-done.19.arrived = bf16[1,272,1024]{2,1,0:T(8,128)(2,1)S(1)} collective-permute-done((bf16[1,272,1024]{2,1,0:T(8,128)(2,1)S(1)}, bf16[1,272,1024]{2,1,0:T(8,128)(2,1)S(1)}, u32[]{:S(2)}, u32[]{:S(2)}) %collective-permute-start.19) | collective-permute-done | bytes 557088 | tf_op jit(solution)/shard_map/ppermute | solution.py:268
  87.1 7.4 collective-permute-done.6.arrived
  101.1 6.4 collective-permute-done.21
  107.6 5.4 collective-permute-done.8
  124.9 6.4 collective-permute-done.24
  131.5 5.4 collective-permute-done.11
  145.1 10.3 %collective-permute-done.33.arrived = bf16[1,272,1024]{2,1,0:T(8,128)(2,1)S(1)} collective-permute-done((bf16[1,272,1024]{2,1,0:T(8,128)(2,1)S(1)}, bf16[1,272,1024]{2,1,0:T(8,128)(2,1)S(1)}, u32[]{:S(2)}, u32[]{:S(2)}) %collective-permute-start.33) | collective-permute-done | bytes 557088 | tf_op jit(solution)/shard_map/ppermute | solution.py:268
  161.0 5.9 collective-permute-done.26.arrived
  173.5 6.4 collective-permute-done.35
  180.1 5.4 collective-permute-done.28
  197.4 6.4 collective-permute-done.38
  217.6 10.3 %collective-permute-done.47.arrived = bf16[1,272,1024]{2,1,0:T(8,128)(2,1)S(1)} collective-permute-done((bf16[1,272,1024]{2,1,0:T(8,128)(2,1)S(1)}, bf16[1,272,1024]{2,1,0:T(8,128)(2,1)S(1)}, u32[]{:S(2)}, u32[]{:S(2)}) %collective-permute-start.47) | collective-permute-done | bytes 557088 | tf_op jit(solution)/shard_map/ppermute | solution.py:268
  233.5 5.9 collective-permute-done.40.arrived
  246.0 6.4 collective-permute-done.49
  252.6 5.4 collective-permute-done.42
  270.7 6.4 collective-permute-done.52
  277.3 5.4 collective-permute-done.45
  291.9 10.1 collective-permute-done.61.arrived
  306.1 7.4 collective-permute-done.54.arrived
  320.1 6.4 collective-permute-done.63
  326.7 5.4 collective-permute-done.56
  343.2 6.4 collective-permute-done.66
  366.8 6.4 collective-permute-done.103
  373.3 5.4 collective-permute-done.69
  378.9 5.8 shard_map.206
  387.4 6.2 shard_map.191
  397.6 6.4 collective-permute-done.106
  404.2 5.4 collective-permute-done.72
  416.5 13.1 %collective-permute-done.108.returned = bf16[1,272,1024]{2,1,0:T(8,128)(2,1)S(1)} collective-permute-done((bf16[1,272,1024]{2,1,0:T(8,128)(2,1)S(1)}, bf16[1,272,1024]{2,1,0:T(8,128)(2,1)S(1)}, u32[]{:S(2)}, u32[]{:S(2)}) %collective-permute-start.108) | collective-permute-done | bytes 557088 | tf_op jit(solution)/shard_map/ppermute | solution.py:268
  433.7 7.5 collective-permute-done.74.returned
  447.2 6.5 collective-permute-done.110
  459.4 5.8 shard_map.209
  467.9 6.0 shard_map.194
  478.0 6.4 collective-permute-done.113
  484.6 5.4 collective-permute-done.79
  497.4 13.2 %collective-permute-done.115.returned = bf16[1,272,1024]{2,1,0:T(8,128)(2,1)S(1)} collective-permute-done((bf16[1,272,1024]{2,1,0:T(8,128)(2,1)S(1)}, bf16[1,272,1024]{2,1,0:T(8,128)(2,1)S(1)}, u32[]{:S(2)}, u32[]{:S(2)}) %collective-permute-start.115) | collective-permute-done | bytes 557088 | tf_op jit(solution)/shard_map/ppermute | solution.py:268
  515.6 6.6 collective-permute-done.81.returned
  528.1 6.4 collective-permute-done.117
  540.3 5.8 shard_map.212
  548.8 6.2 shard_map.197
  559.9 6.4 collective-permute-done.120
  566.5 5.4 collective-permute-done.86
  578.7 13.2 %collective-permute-done.122.returned = bf16[1,272,1024]{2,1,0:T(8,128)(2,1)S(1)} collective-permute-done((bf16[1,272,1024]{2,1,0:T(8,128)(2,1)S(1)}, bf16[1,272,1024]{2,1,0:T(8,128)(2,1)S(1)}, u32[]{:S(2)}, u32[]{:S(2)}) %collective-permute-start.122) | collective-permute-done | bytes 557088 | tf_op jit(solution)/shard_map/ppermute | solution.py:268
  596.8 6.6 collective-permute-done.88.returned
  609.5 6.5 collective-permute-done.124
  621.7 5.8 shard_map.215
  629.3 6.0 shard_map.200
  638.7 6.4 collective-permute-done.127
  645.2 5.4 collective-permute-done.93
  658.1 13.1 %collective-permute-done.129.returned = bf16[1,272,1024]{2,1,0:T(8,128)(2,1)S(1)} collective-permute-done((bf16[1,272,1024]{2,1,0:T(8,128)(2,1)S(1)}, bf16[1,272,1024]{2,1,0:T(8,128)(2,1)S(1)}, u32[]{:S(2)}, u32[]{:S(2)}) %collective-permute-start.129) | collective-permute-done | bytes 557088 | tf_op jit(solution)/shard_map/ppermute | solution.py:268
  674.7 8.0 collective-permute-done.95.returned
  702.0 11.7 %shard_map.223 = bf16[2,1024,512]{2,1,0:T(8,128)(2,1)S(1)} custom-call(bf16[272,1024]{1,0:T(8,128)(2,1)S(1)} %copy-done.386, bf16[272,1024]{1,0:T(8,128)(2,1)S(1)} %copy-done.388, bf16[272,1024]{1,0:T(8,128)(2,1)S(1)} %copy-done.378, bf16[272,1024]{1,0:T(8,128)(2,1)S(1)} %copy-done.380, bf16[272,1024]{1,0:T(8,128)(2,1)S(1)} %copy-done.370, ...), custom_call_target="tpu_custom_call" | custom-call | flops 5704253440 | bytes 13238272 | tf_op jit(solution)/shard_map/pallas_call | solution.py:232
  725.7 12.1 %shard_map.222 = bf16[2,1024,512]{2,1,0:T(8,128)(2,1)S(1)} custom-call(bf16[272,1024]{1,0:T(8,128)(2,1)S(1)} %copy-done.382, bf16[272,1024]{1,0:T(8,128)(2,1)S(1)} %copy-done.384, bf16[272,1024]{1,0:T(8,128)(2,1)S(1)} %copy-done.374, bf16[272,1024]{1,0:T(8,128)(2,1)S(1)} %copy-done.376, bf16[272,1024]{1,0:T(8,128)(2,1)S(1)} %copy-done.366, ...), custom_call_target="tpu_custom_call" | custom-call | flops 5704253440 | bytes 13238272 | tf_op jit(solution)/shard_map/pallas_call | solution.py:232
  738.1 5.8 shard_map.218
  746.2 5.7 shard_map.203
  761.8 9.4 shard_map.220
  783.1 8.8 copy.20
  795.5 6.8 collective-permute-done.134
  815.2 21.3 %all-reduce.2 = (bf16[1,8,1024]{2,1,0:T(8,128)(2,1)S(1)}, bf16[1,2,256]{2,1,0:T(2,128)(2,1)S(1)}, bf16[1,1024]{1,0:T(2,128)(2,1)S(1)}) all-reduce(bf16[1,8,1024]{2,1,0:T(8,128)(2,1)S(1)} %maximum_bitcast_fusion.3, bf16[1,2,256]{2,1,0:T(2,128)(2,1)S(1)} %fusion.4, ...), channel_id=1, replica_groups=mesh['section'=2,'tensor'=4,'dp'=4] {'dp'}, use_global_device_ids=true, to_apply=%region_0.1 | all-reduce | flops 9728 | bytes 38912 | tf_op jit(solution)/shard_map/psum | solution.py:357
  843.6 8.0 copy.21
  851.6 146.2 %all-reduce.6.cloned.1.call-done = (bf16[1,3,1024,256]{3,2,1,0:T(8,128)(2,1)}, bf16[2,256,512]{2,1,0:T(8,128)(2,1)}, bf16[2,1024,512]{2,1,0:T(8,128)(2,1)}, bf16[2,1024,512]{2,1,0:T(8,128)(2,1)}) async-done(((bf16[1,3,1024,256]{3,2,1,0:T(8,128)(2,1)}, bf16[2,256,512]{2,1,0:T(8,128)(2,1)}, bf16[2,1024,512]{2,1,0:T(8,128)(2,1)}, bf16[2,1024,512]{2,1,0:T(8,128)(2,1)}), (bf16[1,3,1024,256]{3,2,1,0:T(8,128)(2,1)}, ...) | async-done | bytes 6291472 | tf_op jit(solution)/shard_map/psum | solution.py:357
  (1194 shorter events, 384.6 us)
Async XLA Ops:
  7.2 990.6 %all-reduce.6.cloned.1.call-start = ((), (), s32[]{:S(2)}) async-start(), calls=%async_computation | async-start | bytes 12582912 | tf_op jit(solution)/shard_map/psum | solution.py:357
  25.4 10.5 %collective-permute-start.14 = (bf16[272,512]{1,0:T(8,128)(2,1)S(1)}, bf16[272,512]{1,0:T(8,128)(2,1)S(1)}, u32[]{:S(2)}, u32[]{:S(2)}) collective-permute-start(bf16[272,512]{1,0:T(8,128)(2,1)S(1)} %add_convert_fusion.71), channel_id=1, source_target_pairs={{0,8},{4,12},{8,0},{12,4},{1,9},{5,13},{9,1},{13,5},{2,10},{6,14},... | collective-permute-start | bytes 835592 | tf_op jit(solution)/shard_map/ppermute | solution.py:250
  28.5 12.7 %collective-permute-start.1 = (bf16[272,512]{1,0:T(8,128)(2,1)S(1)}, bf16[272,512]{1,0:T(8,128)(2,1)S(1)}, u32[]{:S(2)}, u32[]{:S(2)}) collective-permute-start(bf16[272,512]{1,0:T(8,128)(2,1)S(1)} %add_convert_fusion.79), channel_id=1, source_target_pairs={{0,8},{4,12},{8,0},{12,4},{1,9},{5,13},{9,1},{13,5},{2,10},{6,14},... | collective-permute-start | bytes 835592 | tf_op jit(solution)/shard_map/ppermute | solution.py:250
  50.1 9.5 collective-permute-start.17
  51.9 13.2 %collective-permute-start.4 = (bf16[272,512]{1,0:T(8,128)(2,1)S(1)}, bf16[272,512]{1,0:T(8,128)(2,1)S(1)}, u32[]{:S(2)}, u32[]{:S(2)}) collective-permute-start(bf16[272,512]{1,0:T(8,128)(2,1)S(1)} %add_convert_fusion.77), channel_id=1, source_target_pairs={{0,8},{4,12},{8,0},{12,4},{1,9},{5,13},{9,1},{13,5},{2,10},{6,14},... | collective-permute-start | bytes 835592 | tf_op jit(solution)/shard_map/ppermute | solution.py:250
  66.4 16.5 %collective-permute-start.19 = (bf16[1,272,1024]{2,1,0:T(8,128)(2,1)S(1)}, bf16[1,272,1024]{2,1,0:T(8,128)(2,1)S(1)}, u32[]{:S(2)}, u32[]{:S(2)}) collective-permute-start(bf16[1,272,1024]{2,1,0:T(8,128)(2,1)S(1)} %shard_map.168), channel_id=1, source_target_pairs={{0,16},{1,17},{2,18},{3,19},{4,20},{5,21},{6,22},{7,23},{8,24},{9,... | collective-permute-start | bytes 1671176 | tf_op jit(solution)/shard_map/ppermute | solution.py:268
  71.1 23.4 %collective-permute-start.6 = (bf16[1,272,1024]{2,1,0:T(8,128)(2,1)S(1)}, bf16[1,272,1024]{2,1,0:T(8,128)(2,1)S(1)}, u32[]{:S(2)}, u32[]{:S(2)}) collective-permute-start(bf16[1,272,1024]{2,1,0:T(8,128)(2,1)S(1)} %shard_map.162), channel_id=1, source_target_pairs={{0,16},{1,17},{2,18},{3,19},{4,20},{5,21},{6,22},{7,23},{8,24},{9,... | collective-permute-start | bytes 1671176 | tf_op jit(solution)/shard_map/ppermute | solution.py:268
  87.1 10.8 %collective-permute-start.20 = (bf16[272,512]{1,0:T(8,128)(2,1)S(1)}, bf16[272,512]{1,0:T(8,128)(2,1)S(1)}, u32[]{:S(2)}, u32[]{:S(2)}) collective-permute-start(bf16[272,512]{1,0:T(8,128)(2,1)S(1)} %get-tuple-element.294), channel_id=1, source_target_pairs={{0,4},{4,0},{8,12},{12,8},{1,5},{5,1},{9,13},{13,9},{2,6},{6,2},{1... | collective-permute-start | bytes 835592 | tf_op jit(solution)/shard_map/ppermute | solution.py:250
  97.9 9.5 collective-permute-start.21
  99.6 13.4 %collective-permute-start.8 = (bf16[272,512]{1,0:T(8,128)(2,1)S(1)}, bf16[272,512]{1,0:T(8,128)(2,1)S(1)}, u32[]{:S(2)}, u32[]{:S(2)}) collective-permute-start(bf16[272,512]{1,0:T(8,128)(2,1)S(1)} %add_convert_fusion.75), channel_id=1, source_target_pairs={{0,8},{4,12},{8,0},{12,4},{1,9},{5,13},{9,1},{13,5},{2,10},{6,14},... | collective-permute-start | bytes 835592 | tf_op jit(solution)/shard_map/ppermute | solution.py:250
  121.8 9.5 collective-permute-start.24
  123.5 13.4 %collective-permute-start.11 = (bf16[272,512]{1,0:T(8,128)(2,1)S(1)}, bf16[272,512]{1,0:T(8,128)(2,1)S(1)}, u32[]{:S(2)}, u32[]{:S(2)}) collective-permute-start(bf16[272,512]{1,0:T(8,128)(2,1)S(1)} %add_convert_fusion.73), channel_id=1, source_target_pairs={{0,8},{4,12},{8,0},{12,4},{1,9},{5,13},{9,1},{13,5},{2,10},{6,14},... | collective-permute-start | bytes 835592 | tf_op jit(solution)/shard_map/ppermute | solution.py:250
  138.1 17.3 %collective-permute-start.33 = (bf16[1,272,1024]{2,1,0:T(8,128)(2,1)S(1)}, bf16[1,272,1024]{2,1,0:T(8,128)(2,1)S(1)}, u32[]{:S(2)}, u32[]{:S(2)}) collective-permute-start(bf16[1,272,1024]{2,1,0:T(8,128)(2,1)S(1)} %shard_map.171), channel_id=1, source_target_pairs={{0,16},{1,17},{2,18},{3,19},{4,20},{5,21},{6,22},{7,23},{8,24},{9,... | collective-permute-start | bytes 1671176 | tf_op jit(solution)/shard_map/ppermute | solution.py:268
  143.6 23.4 %collective-permute-start.26 = (bf16[1,272,1024]{2,1,0:T(8,128)(2,1)S(1)}, bf16[1,272,1024]{2,1,0:T(8,128)(2,1)S(1)}, u32[]{:S(2)}, u32[]{:S(2)}) collective-permute-start(bf16[1,272,1024]{2,1,0:T(8,128)(2,1)S(1)} %shard_map.165), channel_id=1, source_target_pairs={{0,16},{1,17},{2,18},{3,19},{4,20},{5,21},{6,22},{7,23},{8,24},{9,... | collective-permute-start | bytes 1671176 | tf_op jit(solution)/shard_map/ppermute | solution.py:268
  170.4 9.5 collective-permute-start.35
  172.1 13.4 %collective-permute-start.28 = (bf16[272,512]{1,0:T(8,128)(2,1)S(1)}, bf16[272,512]{1,0:T(8,128)(2,1)S(1)}, u32[]{:S(2)}, u32[]{:S(2)}) collective-permute-start(bf16[272,512]{1,0:T(8,128)(2,1)S(1)} %add_convert_fusion.63), channel_id=1, source_target_pairs={{0,8},{4,12},{8,0},{12,4},{1,9},{5,13},{9,1},{13,5},{2,10},{6,14},... | collective-permute-start | bytes 835592 | tf_op jit(solution)/shard_map/ppermute | solution.py:250
  194.3 9.5 collective-permute-start.38
  195.9 13.4 %collective-permute-start.31 = (bf16[272,512]{1,0:T(8,128)(2,1)S(1)}, bf16[272,512]{1,0:T(8,128)(2,1)S(1)}, u32[]{:S(2)}, u32[]{:S(2)}) collective-permute-start(bf16[272,512]{1,0:T(8,128)(2,1)S(1)} %add_convert_fusion.61), channel_id=1, source_target_pairs={{0,8},{4,12},{8,0},{12,4},{1,9},{5,13},{9,1},{13,5},{2,10},{6,14},... | collective-permute-start | bytes 835592 | tf_op jit(solution)/shard_map/ppermute | solution.py:250
  210.6 17.3 %collective-permute-start.47 = (bf16[1,272,1024]{2,1,0:T(8,128)(2,1)S(1)}, bf16[1,272,1024]{2,1,0:T(8,128)(2,1)S(1)}, u32[]{:S(2)}, u32[]{:S(2)}) collective-permute-start(bf16[1,272,1024]{2,1,0:T(8,128)(2,1)S(1)} %shard_map.177), channel_id=1, source_target_pairs={{0,16},{1,17},{2,18},{3,19},{4,20},{5,21},{6,22},{7,23},{8,24},{9,... | collective-permute-start | bytes 1671176 | tf_op jit(solution)/shard_map/ppermute | solution.py:268
  216.1 23.4 %collective-permute-start.40 = (bf16[1,272,1024]{2,1,0:T(8,128)(2,1)S(1)}, bf16[1,272,1024]{2,1,0:T(8,128)(2,1)S(1)}, u32[]{:S(2)}, u32[]{:S(2)}) collective-permute-start(bf16[1,272,1024]{2,1,0:T(8,128)(2,1)S(1)} %shard_map.174), channel_id=1, source_target_pairs={{0,16},{1,17},{2,18},{3,19},{4,20},{5,21},{6,22},{7,23},{8,24},{9,... | collective-permute-start | bytes 1671176 | tf_op jit(solution)/shard_map/ppermute | solution.py:268
  242.9 9.5 collective-permute-start.49
  244.6 13.4 %collective-permute-start.42 = (bf16[272,512]{1,0:T(8,128)(2,1)S(1)}, bf16[272,512]{1,0:T(8,128)(2,1)S(1)}, u32[]{:S(2)}, u32[]{:S(2)}) collective-permute-start(bf16[272,512]{1,0:T(8,128)(2,1)S(1)} %add_convert_fusion.55), channel_id=1, source_target_pairs={{0,8},{4,12},{8,0},{12,4},{1,9},{5,13},{9,1},{13,5},{2,10},{6,14},... | collective-permute-start | bytes 835592 | tf_op jit(solution)/shard_map/ppermute | solution.py:250
  267.6 9.5 collective-permute-start.52
  269.2 13.4 %collective-permute-start.45 = (bf16[272,512]{1,0:T(8,128)(2,1)S(1)}, bf16[272,512]{1,0:T(8,128)(2,1)S(1)}, u32[]{:S(2)}, u32[]{:S(2)}) collective-permute-start(bf16[272,512]{1,0:T(8,128)(2,1)S(1)} %add_convert_fusion.53), channel_id=1, source_target_pairs={{0,8},{4,12},{8,0},{12,4},{1,9},{5,13},{9,1},{13,5},{2,10},{6,14},... | collective-permute-start | bytes 835592 | tf_op jit(solution)/shard_map/ppermute | solution.py:250
  284.7 17.3 %collective-permute-start.61 = (bf16[1,272,1024]{2,1,0:T(8,128)(2,1)S(1)}, bf16[1,272,1024]{2,1,0:T(8,128)(2,1)S(1)}, u32[]{:S(2)}, u32[]{:S(2)}) collective-permute-start(bf16[1,272,1024]{2,1,0:T(8,128)(2,1)S(1)} %shard_map.183), channel_id=1, source_target_pairs={{0,16},{1,17},{2,18},{3,19},{4,20},{5,21},{6,22},{7,23},{8,24},{9,... | collective-permute-start | bytes 1671176 | tf_op jit(solution)/shard_map/ppermute | solution.py:268
  290.1 23.4 %collective-permute-start.54 = (bf16[1,272,1024]{2,1,0:T(8,128)(2,1)S(1)}, bf16[1,272,1024]{2,1,0:T(8,128)(2,1)S(1)}, u32[]{:S(2)}, u32[]{:S(2)}) collective-permute-start(bf16[1,272,1024]{2,1,0:T(8,128)(2,1)S(1)} %shard_map.180), channel_id=1, source_target_pairs={{0,16},{1,17},{2,18},{3,19},{4,20},{5,21},{6,22},{7,23},{8,24},{9,... | collective-permute-start | bytes 1671176 | tf_op jit(solution)/shard_map/ppermute | solution.py:268
  306.1 10.8 %collective-permute-start.62 = (bf16[272,512]{1,0:T(8,128)(2,1)S(1)}, bf16[272,512]{1,0:T(8,128)(2,1)S(1)}, u32[]{:S(2)}, u32[]{:S(2)}) collective-permute-start(bf16[272,512]{1,0:T(8,128)(2,1)S(1)} %get-tuple-element.324), channel_id=1, source_target_pairs={{0,4},{4,0},{8,12},{12,8},{1,5},{5,1},{9,13},{13,9},{2,6},{6,2},{1... | collective-permute-start | bytes 835592 | tf_op jit(solution)/shard_map/ppermute | solution.py:250
  317.0 9.5 collective-permute-start.63
  318.6 13.4 %collective-permute-start.56 = (bf16[272,512]{1,0:T(8,128)(2,1)S(1)}, bf16[272,512]{1,0:T(8,128)(2,1)S(1)}, u32[]{:S(2)}, u32[]{:S(2)}) collective-permute-start(bf16[272,512]{1,0:T(8,128)(2,1)S(1)} %add_convert_fusion.47), channel_id=1, source_target_pairs={{0,8},{4,12},{8,0},{12,4},{1,9},{5,13},{9,1},{13,5},{2,10},{6,14},... | collective-permute-start | bytes 835592 | tf_op jit(solution)/shard_map/ppermute | solution.py:250
  340.1 9.5 collective-permute-start.66
  341.7 13.4 %collective-permute-start.59 = (bf16[272,512]{1,0:T(8,128)(2,1)S(1)}, bf16[272,512]{1,0:T(8,128)(2,1)S(1)}, u32[]{:S(2)}, u32[]{:S(2)}) collective-permute-start(bf16[272,512]{1,0:T(8,128)(2,1)S(1)} %add_convert_fusion.45), channel_id=1, source_target_pairs={{0,8},{4,12},{8,0},{12,4},{1,9},{5,13},{9,1},{13,5},{2,10},{6,14},... | collective-permute-start | bytes 835592 | tf_op jit(solution)/shard_map/ppermute | solution.py:250
  363.7 9.5 collective-permute-start.103
  365.3 13.4 %collective-permute-start.69 = (bf16[272,512]{1,0:T(8,128)(2,1)S(1)}, bf16[272,512]{1,0:T(8,128)(2,1)S(1)}, u32[]{:S(2)}, u32[]{:S(2)}) collective-permute-start(bf16[272,512]{1,0:T(8,128)(2,1)S(1)} %add_convert_fusion.39), channel_id=1, source_target_pairs={{0,8},{4,12},{8,0},{12,4},{1,9},{5,13},{9,1},{13,5},{2,10},{6,14},... | collective-permute-start | bytes 835592 | tf_op jit(solution)/shard_map/ppermute | solution.py:250
  394.5 9.5 collective-permute-start.106
  396.2 13.4 %collective-permute-start.72 = (bf16[272,512]{1,0:T(8,128)(2,1)S(1)}, bf16[272,512]{1,0:T(8,128)(2,1)S(1)}, u32[]{:S(2)}, u32[]{:S(2)}) collective-permute-start(bf16[272,512]{1,0:T(8,128)(2,1)S(1)} %add_convert_fusion.37), channel_id=1, source_target_pairs={{0,8},{4,12},{8,0},{12,4},{1,9},{5,13},{9,1},{13,5},{2,10},{6,14},... | collective-permute-start | bytes 835592 | tf_op jit(solution)/shard_map/ppermute | solution.py:250
  412.3 17.3 %collective-permute-start.108 = (bf16[1,272,1024]{2,1,0:T(8,128)(2,1)S(1)}, bf16[1,272,1024]{2,1,0:T(8,128)(2,1)S(1)}, u32[]{:S(2)}, u32[]{:S(2)}) collective-permute-start(bf16[1,272,1024]{2,1,0:T(8,128)(2,1)S(1)} %get-tuple-element.381), channel_id=1, source_target_pairs={{16,0},{17,1},{18,2},{19,3},{20,4},{21,5},{22,6},{23,7},{24,8},{25... | collective-permute-start | bytes 1671176 | tf_op jit(solution)/shard_map/ppermute | solution.py:268
  415.2 26.1 %collective-permute-start.74 = (bf16[1,272,1024]{2,1,0:T(8,128)(2,1)S(1)}, bf16[1,272,1024]{2,1,0:T(8,128)(2,1)S(1)}, u32[]{:S(2)}, u32[]{:S(2)}) collective-permute-start(bf16[1,272,1024]{2,1,0:T(8,128)(2,1)S(1)} %get-tuple-element.335), channel_id=1, source_target_pairs={{16,0},{17,1},{18,2},{19,3},{20,4},{21,5},{22,6},{23,7},{24,8},{25... | collective-permute-start | bytes 1671176 | tf_op jit(solution)/shard_map/ppermute | solution.py:268
  433.7 10.3 %collective-permute-start.109 = (bf16[272,512]{1,0:T(8,128)(2,1)S(1)}, bf16[272,512]{1,0:T(8,128)(2,1)S(1)}, u32[]{:S(2)}, u32[]{:S(2)}) collective-permute-start(bf16[272,512]{1,0:T(8,128)(2,1)S(1)} %get-tuple-element.385), channel_id=1, source_target_pairs={{0,4},{4,0},{8,12},{12,8},{1,5},{5,1},{9,13},{13,9},{2,6},{6,2},{1... | collective-permute-start | bytes 835592 | tf_op jit(solution)/shard_map/ppermute | solution.py:250
  444.2 9.5 collective-permute-start.110
  445.8 13.4 %collective-permute-start.76 = (bf16[272,512]{1,0:T(8,128)(2,1)S(1)}, bf16[272,512]{1,0:T(8,128)(2,1)S(1)}, u32[]{:S(2)}, u32[]{:S(2)}) collective-permute-start(bf16[272,512]{1,0:T(8,128)(2,1)S(1)} %add_convert_fusion.35), channel_id=1, source_target_pairs={{0,8},{4,12},{8,0},{12,4},{1,9},{5,13},{9,1},{13,5},{2,10},{6,14},... | collective-permute-start | bytes 835592 | tf_op jit(solution)/shard_map/ppermute | solution.py:250
  474.9 9.5 collective-permute-start.113
  476.6 13.4 %collective-permute-start.79 = (bf16[272,512]{1,0:T(8,128)(2,1)S(1)}, bf16[272,512]{1,0:T(8,128)(2,1)S(1)}, u32[]{:S(2)}, u32[]{:S(2)}) collective-permute-start(bf16[272,512]{1,0:T(8,128)(2,1)S(1)} %add_convert_fusion.33), channel_id=1, source_target_pairs={{0,8},{4,12},{8,0},{12,4},{1,9},{5,13},{9,1},{13,5},{2,10},{6,14},... | collective-permute-start | bytes 835592 | tf_op jit(solution)/shard_map/ppermute | solution.py:250
  493.3 17.3 %collective-permute-start.115 = (bf16[1,272,1024]{2,1,0:T(8,128)(2,1)S(1)}, bf16[1,272,1024]{2,1,0:T(8,128)(2,1)S(1)}, u32[]{:S(2)}, u32[]{:S(2)}) collective-permute-start(bf16[1,272,1024]{2,1,0:T(8,128)(2,1)S(1)} %get-tuple-element.390), channel_id=1, source_target_pairs={{16,0},{17,1},{18,2},{19,3},{20,4},{21,5},{22,6},{23,7},{24,8},{25... | collective-permute-start | bytes 1671176 | tf_op jit(solution)/shard_map/ppermute | solution.py:268
  496.1 26.0 %collective-permute-start.81 = (bf16[1,272,1024]{2,1,0:T(8,128)(2,1)S(1)}, bf16[1,272,1024]{2,1,0:T(8,128)(2,1)S(1)}, u32[]{:S(2)}, u32[]{:S(2)}) collective-permute-start(bf16[1,272,1024]{2,1,0:T(8,128)(2,1)S(1)} %get-tuple-element.344), channel_id=1, source_target_pairs={{16,0},{17,1},{18,2},{19,3},{20,4},{21,5},{22,6},{23,7},{24,8},{25... | collective-permute-start | bytes 1671176 | tf_op jit(solution)/shard_map/ppermute | solution.py:268
  525.1 9.5 collective-permute-start.117
  526.7 13.4 %collective-permute-start.83 = (bf16[272,512]{1,0:T(8,128)(2,1)S(1)}, bf16[272,512]{1,0:T(8,128)(2,1)S(1)}, u32[]{:S(2)}, u32[]{:S(2)}) collective-permute-start(bf16[272,512]{1,0:T(8,128)(2,1)S(1)} %add_convert_fusion.31), channel_id=1, source_target_pairs={{0,8},{4,12},{8,0},{12,4},{1,9},{5,13},{9,1},{13,5},{2,10},{6,14},... | collective-permute-start | bytes 835592 | tf_op jit(solution)/shard_map/ppermute | solution.py:250
  556.8 9.5 collective-permute-start.120
  558.5 13.4 %collective-permute-start.86 = (bf16[272,512]{1,0:T(8,128)(2,1)S(1)}, bf16[272,512]{1,0:T(8,128)(2,1)S(1)}, u32[]{:S(2)}, u32[]{:S(2)}) collective-permute-start(bf16[272,512]{1,0:T(8,128)(2,1)S(1)} %add_convert_fusion.29), channel_id=1, source_target_pairs={{0,8},{4,12},{8,0},{12,4},{1,9},{5,13},{9,1},{13,5},{2,10},{6,14},... | collective-permute-start | bytes 835592 | tf_op jit(solution)/shard_map/ppermute | solution.py:250
  574.6 17.3 %collective-permute-start.122 = (bf16[1,272,1024]{2,1,0:T(8,128)(2,1)S(1)}, bf16[1,272,1024]{2,1,0:T(8,128)(2,1)S(1)}, u32[]{:S(2)}, u32[]{:S(2)}) collective-permute-start(bf16[1,272,1024]{2,1,0:T(8,128)(2,1)S(1)} %get-tuple-element.399), channel_id=1, source_target_pairs={{16,0},{17,1},{18,2},{19,3},{20,4},{21,5},{22,6},{23,7},{24,8},{25... | collective-permute-start | bytes 1671176 | tf_op jit(solution)/shard_map/ppermute | solution.py:268
  577.4 26.0 %collective-permute-start.88 = (bf16[1,272,1024]{2,1,0:T(8,128)(2,1)S(1)}, bf16[1,272,1024]{2,1,0:T(8,128)(2,1)S(1)}, u32[]{:S(2)}, u32[]{:S(2)}) collective-permute-start(bf16[1,272,1024]{2,1,0:T(8,128)(2,1)S(1)} %get-tuple-element.353), channel_id=1, source_target_pairs={{16,0},{17,1},{18,2},{19,3},{20,4},{21,5},{22,6},{23,7},{24,8},{25... | collective-permute-start | bytes 1671176 | tf_op jit(solution)/shard_map/ppermute | solution.py:268
  606.4 9.5 collective-permute-start.124
  608.0 13.4 %collective-permute-start.90 = (bf16[272,512]{1,0:T(8,128)(2,1)S(1)}, bf16[272,512]{1,0:T(8,128)(2,1)S(1)}, u32[]{:S(2)}, u32[]{:S(2)}) collective-permute-start(bf16[272,512]{1,0:T(8,128)(2,1)S(1)} %add_convert_fusion.27), channel_id=1, source_target_pairs={{0,8},{4,12},{8,0},{12,4},{1,9},{5,13},{9,1},{13,5},{2,10},{6,14},... | collective-permute-start | bytes 835592 | tf_op jit(solution)/shard_map/ppermute | solution.py:250
  635.5 9.5 collective-permute-start.127
  637.2 13.4 %collective-permute-start.93 = (bf16[272,512]{1,0:T(8,128)(2,1)S(1)}, bf16[272,512]{1,0:T(8,128)(2,1)S(1)}, u32[]{:S(2)}, u32[]{:S(2)}) collective-permute-start(bf16[272,512]{1,0:T(8,128)(2,1)S(1)} %add_convert_fusion.25), channel_id=1, source_target_pairs={{0,8},{4,12},{8,0},{12,4},{1,9},{5,13},{9,1},{13,5},{2,10},{6,14},... | collective-permute-start | bytes 835592 | tf_op jit(solution)/shard_map/ppermute | solution.py:250
  653.9 17.3 %collective-permute-start.129 = (bf16[1,272,1024]{2,1,0:T(8,128)(2,1)S(1)}, bf16[1,272,1024]{2,1,0:T(8,128)(2,1)S(1)}, u32[]{:S(2)}, u32[]{:S(2)}) collective-permute-start(bf16[1,272,1024]{2,1,0:T(8,128)(2,1)S(1)} %get-tuple-element.408), channel_id=1, source_target_pairs={{16,0},{17,1},{18,2},{19,3},{20,4},{21,5},{22,6},{23,7},{24,8},{25... | collective-permute-start | bytes 1671176 | tf_op jit(solution)/shard_map/ppermute | solution.py:268
  656.8 26.0 %collective-permute-start.95 = (bf16[1,272,1024]{2,1,0:T(8,128)(2,1)S(1)}, bf16[1,272,1024]{2,1,0:T(8,128)(2,1)S(1)}, u32[]{:S(2)}, u32[]{:S(2)}) collective-permute-start(bf16[1,272,1024]{2,1,0:T(8,128)(2,1)S(1)} %get-tuple-element.362), channel_id=1, source_target_pairs={{16,0},{17,1},{18,2},{19,3},{20,4},{21,5},{22,6},{23,7},{24,8},{25... | collective-permute-start | bytes 1671176 | tf_op jit(solution)/shard_map/ppermute | solution.py:268
  674.7 12.1 %collective-permute-start.130 = (bf16[272,512]{1,0:T(8,128)(2,1)S(1)}, bf16[272,512]{1,0:T(8,128)(2,1)S(1)}, u32[]{:S(2)}, u32[]{:S(2)}) collective-permute-start(bf16[272,512]{1,0:T(8,128)(2,1)S(1)} %get-tuple-element.412), channel_id=1, source_target_pairs={{0,4},{4,0},{8,12},{12,8},{1,5},{5,1},{9,13},{13,9},{2,6},{6,2},{1... | collective-permute-start | bytes 835592 | tf_op jit(solution)/shard_map/ppermute | solution.py:250
  687.0 26.8 %collective-permute-start.131 = (bf16[272,512]{1,0:T(8,128)(2,1)S(1)}, bf16[272,512]{1,0:T(8,128)(2,1)S(1)}, u32[]{:S(2)}, u32[]{:S(2)}) collective-permute-start(bf16[272,512]{1,0:T(8,128)(2,1)S(1)} %add_convert_fusion.3), channel_id=1, source_target_pairs={{0,8},{4,12},{8,0},{12,4},{1,9},{5,13},{9,1},{13,5},{2,10},{6,14},... | collective-permute-start | bytes 835592 | tf_op jit(solution)/shard_map/ppermute | solution.py:250
  688.6 25.3 %collective-permute-start.97 = (bf16[272,512]{1,0:T(8,128)(2,1)S(1)}, bf16[272,512]{1,0:T(8,128)(2,1)S(1)}, u32[]{:S(2)}, u32[]{:S(2)}) collective-permute-start(bf16[272,512]{1,0:T(8,128)(2,1)S(1)} %add_convert_fusion.23), channel_id=1, source_target_pairs={{0,8},{4,12},{8,0},{12,4},{1,9},{5,13},{9,1},{13,5},{2,10},{6,14},... | collective-permute-start | bytes 835592 | tf_op jit(solution)/shard_map/ppermute | solution.py:250
  713.8 24.0 %collective-permute-start.132 = (bf16[272,512]{1,0:T(8,128)(2,1)S(1)}, bf16[272,512]{1,0:T(8,128)(2,1)S(1)}, u32[]{:S(2)}, u32[]{:S(2)}) collective-permute-start(bf16[272,512]{1,0:T(8,128)(2,1)S(1)} %add_convert_fusion.2.d_m), channel_id=1, source_target_pairs={{0,4},{4,0},{8,12},{12,8},{1,5},{5,1},{9,13},{13,9},{2,6},{6,2},{1... | collective-permute-start | bytes 835592 | tf_op jit(solution)/shard_map/ppermute | solution.py:250
  714.0 32.2 %collective-permute-start.98 = (bf16[272,512]{1,0:T(8,128)(2,1)S(1)}, bf16[272,512]{1,0:T(8,128)(2,1)S(1)}, u32[]{:S(2)}, u32[]{:S(2)}) collective-permute-start(bf16[272,512]{1,0:T(8,128)(2,1)S(1)} %add_convert_fusion.22.d_m), channel_id=1, source_target_pairs={{0,4},{4,0},{8,12},{12,8},{1,5},{5,1},{9,13},{13,9},{2,6},{6,2},{1... | collective-permute-start | bytes 835592 | tf_op jit(solution)/shard_map/ppermute | solution.py:250
  781.8 10.8 %collective-permute-start.133 = (bf16[272,512]{1,0:T(8,128)(2,1)S(1)}, bf16[272,512]{1,0:T(8,128)(2,1)S(1)}, u32[]{:S(2)}, u32[]{:S(2)}) collective-permute-start(bf16[272,512]{1,0:T(8,128)(2,1)S(1)} %copy-done.326), channel_id=1, source_target_pairs={{0,4},{4,0},{8,12},{12,8},{1,5},{5,1},{9,13},{13,9},{2,6},{6,2},{1... | collective-permute-start | bytes 835592 | tf_op jit(solution)/shard_map/ppermute | solution.py:250
  792.7 9.6 collective-permute-start.134
  794.4 13.0 %collective-permute-start.100 = (bf16[272,512]{1,0:T(8,128)(2,1)S(1)}, bf16[272,512]{1,0:T(8,128)(2,1)S(1)}, u32[]{:S(2)}, u32[]{:S(2)}) collective-permute-start(bf16[272,512]{1,0:T(8,128)(2,1)S(1)} %add_convert_fusion.21), channel_id=1, source_target_pairs={{0,8},{4,12},{8,0},{12,4},{1,9},{5,13},{9,1},{13,5},{2,10},{6,14},... | collective-permute-start | bytes 835592 | tf_op jit(solution)/shard_map/ppermute | solution.py:250
  (468 other events, 6255.2 us)
Sparse Core Ops, SparseCore 0:
  772.5 225.2 all-reduce.5

commit v2 on v1

--- a/solution.py
+++ b/solution.py
@@ -51,6 +51,11 @@
     send_ref[...] = jnp.where(low_core, hi, lo).astype(LOW)
 
 
+def own_half(flags, full):
+    half = full.shape[1] // 2
+    return jnp.where(flags[1] == 0, full[:, :half], full[:, half:]).astype(LOW)
+
+
 def join(flags, mine_ref, other_ref):
     low_core = flags[1] == 0
     mine, other = mine_ref[...].astype(F32), other_ref[...].astype(F32)
@@ -67,8 +72,8 @@
     return e * (1.0 / jnp.sum(e, axis=-1, keepdims=True))
 
 
-def attn_fwd_kernel(seq, flags, own, arrived, vec, wqkv, qvb, wout, x_o, n1_o, qkv_o, o_o, mine_o, send_o):
-    x16 = jnp.where(flags[0] == 1, own[0].astype(F32), arrived[0].astype(F32))
+def attn_fwd_kernel(seq, flags, own, arr_m, arr_s, vec, wqkv, qvb, wout, x_o, n1_o, qkv_o, o_o, mine_o, send_o):
+    x16 = jnp.where(flags[0] == 1, own[0].astype(F32), join(flags, arr_m, arr_s))
     x_o[...] = x16.astype(LOW)
     unit, _ = unit_rows_of(x16)
     n1 = (unit * vec[0:1, :] + vec[1:2, :]).astype(LOW)
@@ -112,13 +117,15 @@
     split_out(flags, total, mine_o, send_o)
 
 
-def out_kernel(flags, x, a_m, a_s, m_m, m_s, vec, y_o):
+def out_kernel(flags, x, a_m, a_s, m_m, m_s, vec, y_o, half_o):
     h1 = x[...].astype(F32) + vec[3:4, :] * (join(flags, a_m, a_s) + vec[2:3, :])
-    y_o[0] = (h1 + vec[7:8, :] * (join(flags, m_m, m_s) + vec[6:7, :])).astype(LOW)
-
-
-def mlp_bwd_kernel(flags, cot, returned, m_m, m_s, dg, vec, fc1, fc2, dy_o, dm_o, du_o, mine_o, send_o, sums_o):
-    dy = jnp.where(flags[0] == 1, returned[0].astype(F32), cot[0].astype(F32))
+    y = h1 + vec[7:8, :] * (join(flags, m_m, m_s) + vec[6:7, :])
+    y_o[...] = y.astype(LOW)
+    half_o[...] = own_half(flags, y)
+
+
+def mlp_bwd_kernel(flags, cot, ret_m, ret_s, m_m, m_s, dg, vec, fc1, fc2, dy_o, dm_o, du_o, mine_o, send_o, sums_o):
+    dy = jnp.where(flags[0] == 1, join(flags, ret_m, ret_s), cot[0].astype(F32))
     dy_o[...] = dy.astype(LOW)
     m = join(flags, m_m, m_s)
     scaled = dy * vec[7:8, :]
@@ -187,11 +194,11 @@
     sums_o[1:2, :] = col_sum(dn1)
     dx = dh[...] + norm_back(dn1, unit, inverse, vec[0:1, :])
     dx_o[...] = dx[: dx_o.shape[0]]
-    low_o[0] = dx.astype(LOW)
+    low_o[...] = own_half(flags, dx)
 
 
 def weight_kernel(count, *refs):
-    lefts, rights, out = refs[:count], refs[count : 2 * count], refs[2 * count]
+    lefts, rights, out = refs[:count], refs[count : 2 * count], refs[2 * count + 1]
     total = dot_tn(lefts[0][...], rights[0][...])
     for n in range(1, count):
         total = total + dot_tn(lefts[n][...], rights[n][...])
@@ -204,7 +211,11 @@
     return pl.BlockSpec(block, lambda i: at)
 
 
-def call(kernel, args, outs, picks=None, flops=0):
+def skip_last(kernel, at, *refs):
+    kernel(*refs[:at], *refs[at + 1 :])
+
+
+def call(kernel, args, outs, after, picks=None, flops=0):
     picks = picks or {}
     specs = [pl.BlockSpec(memory_space=pltpu.SMEM)]
     for n, arg in enumerate(args[1:], 1):
@@ -212,19 +223,20 @@
             specs.append(whole(arg.shape, (1,) + arg.shape[1:], (picks[n], 0, 0)))
         else:
             specs.append(whole(arg.shape))
+    specs.append(pl.BlockSpec(memory_space=pl.ANY))
     moved = sum(a.size * a.dtype.itemsize for a in args[1:])
     return pl.pallas_call(
-        kernel,
+        partial(skip_last, kernel, len(args)),
         grid=(1,),
         in_specs=specs,
         out_specs=[whole(s.shape) for s in outs],
         out_shape=outs,
         compiler_params=pltpu.CompilerParams(vmem_limit_bytes=VMEM_BYTES),
         cost_estimate=pl.CostEstimate(flops=flops, bytes_accessed=moved, transcendentals=0),
-    )(*args)
-
-
-def weight_grad(lefts, rights, blocks):
+    )(*args, after)
+
+
+def weight_grad(lefts, rights, blocks, after):
     count = len(lefts)
     rows, depth = lefts[0].shape
     width = rights[0].shape[1]
@@ -233,7 +245,8 @@
         partial(weight_kernel, count),
         grid=(blocks,),
         in_specs=[pl.BlockSpec((rows, depth), lambda i: (0, 0))] * count
-        + [pl.BlockSpec((rows, block), lambda i: (0, i))] * count,
+        + [pl.BlockSpec((rows, block), lambda i: (0, i))] * count
+        + [pl.BlockSpec(memory_space=pl.ANY)],
         out_specs=pl.BlockSpec((1, depth, block), lambda i: (i, 0, 0)),
         out_shape=jax.ShapeDtypeStruct((blocks, depth, block), LOW),
         compiler_params=pltpu.CompilerParams(vmem_limit_bytes=VMEM_BYTES),
@@ -242,7 +255,21 @@
             bytes_accessed=2 * count * rows * (depth + width) + 2 * depth * width,
             transcendentals=0,
         ),
-    )(*lefts, *rights)
+    )(*lefts, *rights, after)
+
+
+def pass_kernel(value, after, out):
+    pass
+
+
+def held_until(value, after):
+    return pl.pallas_call(
+        pass_kernel,
+        in_specs=[pl.BlockSpec(memory_space=pl.ANY)] * 2,
+        out_specs=pl.BlockSpec(memory_space=pl.ANY),
+        out_shape=jax.ShapeDtypeStruct(value.shape, value.dtype),
+        input_output_aliases={0: 0},
+    )(value, after)
 
 
 def swap(value, bit):
@@ -253,19 +280,20 @@
 def tensor_sum(mine, send):
     size = lax.axis_size("tensor")
     got = swap(send, 1)
-    held = (mine.astype(F32) + got.astype(F32)).astype(LOW)
+    first = held = (mine.astype(F32) + got.astype(F32)).astype(LOW)
     bit = 2
     while bit < size:
         got = swap(held, bit)
         held = (held.astype(F32) + got.astype(F32)).astype(LOW)
         bit *= 2
-    return held, swap(held, 1)
+    return held, swap(held, 1), first
 
 
 def passed_along(block, distance):
     devices = range(lax.axis_size("section"))
     route = [(i - distance, i) for i in devices if i - distance in devices]
-    return lax.ppermute(block, "section", route)
+    arrived = lax.ppermute(block, "section", route)
+    return arrived, swap(arrived, 1)
 
 
 def body(tokens, cotangent, vectors, w_qkv, qv_bias, w_out, w_fc1, fc1_bias, w_fc2):
@@ -283,6 +311,8 @@
     own = jnp.pad(tokens.reshape(units, seq, width), pad)
     cot = jnp.pad(cotangent.reshape(units, seq, width), pad)
     zeros = jnp.zeros((1, rows, width), LOW)
+    nothing = (jnp.zeros((rows, width // 2), LOW),) * 2
+    last = nothing[0]
 
     def low(*shape):
         return jax.ShapeDtypeStruct(shape, LOW)
@@ -294,80 +324,125 @@
     ticks = units + LAG
     unit_flops = 2 * rows * width
     arrivals, results, records = {}, [], []
-    for t in range(ticks):
-        x, n1, qkv, o, mine, send = call(
-            partial(attn_fwd_kernel, seq),
-            (flags, own if t < units else zeros, arrivals.get(t, zeros), vec, wqkv, qvb, wout),
-            [low(rows, width), low(rows, width), low(rows, 3 * share), low(rows, share)] + halves,
-            {1: t} if t < units else None,
-            unit_flops * share * 8,
-        )
-        a_m, a_s = tensor_sum(mine, send)
-        n2, g, dg, mine, send = call(
-            mlp_fwd_kernel,
-            (flags, x, a_m, a_s, vec, fc1, fc1b, fc2),
-            [low(rows, width), low(rows, hidden), low(rows, hidden)] + halves,
-            flops=unit_flops * hidden * 3,
-        )
-        m_m, m_s = tensor_sum(mine, send)
-        (y,) = call(out_kernel, (flags, x, a_m, a_s, m_m, m_s, vec), [low(1, rows, width)])
-        results.append(y)
-        if t + LAG < ticks:
-            arrivals[t + LAG] = passed_along(y, 1)
-        records.append((x, n1, qkv, o, a_m, a_s, n2, g, dg, m_m, m_s))
+    for start in range(0, ticks, LAG):
+        group = range(start, min(start + LAG, ticks))
+        kept = {}
+        for t in group:
+            x, n1, qkv, o, mine, send = call(
+                partial(attn_fwd_kernel, seq),
+                (flags, own if t < units else zeros, *arrivals.get(t, nothing), vec, wqkv, qvb, wout),
+                [low(rows, width), low(rows, width), low(rows, 3 * share), low(rows, share)] + halves,
+                last,
+                {1: t} if t < units else None,
+                unit_flops * share * 8,
+            )
+            a_m, a_s, last = tensor_sum(mine, send)
+            kept[t] = (x, n1, qkv, o, a_m, a_s)
+        for t in group:
+            x, n1, qkv, o, a_m, a_s = kept[t]
+            n2, g, dg, mine, send = call(
+                mlp_fwd_kernel,
+                (flags, x, a_m, a_s, vec, fc1, fc1b, fc2),
+                [low(rows, width), low(rows, hidden), low(rows, hidden)] + halves,
+                last,
+                flops=unit_flops * hidden * 3,
+            )
+            m_m, m_s, last = tensor_sum(mine, send)
+            kept[t] += (n2, g, dg, m_m, m_s)
+        for t in group:
+            x, a_m, a_s, m_m, m_s = [kept[t][n] for n in (0, 4, 5, 9, 10)]
+            y, half = call(
+                out_kernel,
+                (flags, x, a_m, a_s, m_m, m_s, vec),
+                [low(rows, width), low(rows, width // 2)],
+                last,
+            )
+            results.append(y)
+            if t + LAG < ticks:
+                arrivals[t + LAG] = passed_along(half, 1)
+            records.append(kept[t])
 
     returns, grads, small = {}, [], []
     pieces = [[] for _ in range(4)]
-    for t in range(ticks):
-        x, n1, qkv, o, a_m, a_s, n2, g, dg, m_m, m_s = records[ticks - 1 - t]
-        dy, dm, du, mine, send, sums_mlp = call(
-            mlp_bwd_kernel,
-            (flags, cot if t < units else zeros, returns.get(t, zeros), m_m, m_s, dg, vec, fc1, fc2),
-            [low(rows, width), low(rows, width), low(rows, hidden)] + halves + [wide(3, width)],
-            {1: units - 1 - t} if t < units else None,
-            unit_flops * hidden * 2,
-        )
-        d_m, d_s = tensor_sum(mine, send)
-        dh, da, dqkv, mine, send, sums_attn, pair = call(
-            partial(attn_bwd_kernel, seq),
-            (flags, x, a_m, a_s, dy, d_m, d_s, qkv, vec, wqkv, wout),
-            [wide(rows, width), low(rows, width), low(rows, 3 * share)] + halves + [wide(4, width), wide(2, share)],
-            flops=unit_flops * share * 10,
-        )
-        d_m, d_s = tensor_sum(mine, send)
-        dx, dx_low, sums_in = call(
-            in_bwd_kernel,
-            (flags, x, dh, d_m, d_s, vec),
-            [wide(seq, width), low(1, rows, width), wide(2, width)],
-        )
-        grads.append(dx)
-        if t + LAG < ticks:
-            returns[t + LAG] = passed_along(dx_low, -1)
-        small.append((sums_mlp, sums_attn, sums_in, pair))
-        for piece, pairing in zip(pieces, ((g, dm), (n2, du), (o, da), (n1, dqkv))):
-            piece.append(pairing)
-
-    blocks = (2, 2, 2, 3)
-    grad_fc2, grad_fc1, grad_out, grad_qkv = [
-        weight_grad([p[0] for p in piece], [p[1] for p in piece], n)
-        for piece, n in zip(pieces, blocks)
-    ]
+    for start in range(0, ticks, LAG):
+        group = range(start, min(start + LAG, ticks))
+        kept = {}
+        for t in group:
+            g, dg, m_m, m_s = records[ticks - 1 - t][7:]
+            dy, dm, du, mine, send, sums_mlp = call(
+                mlp_bwd_kernel,
+                (flags, cot if t < units else zeros, *returns.get(t, nothing), m_m, m_s, dg, vec, fc1, fc2),
+                [low(rows, width), low(rows, width), low(rows, hidden)] + halves + [wide(3, width)],
+                last,
+                {1: units - 1 - t} if t < units else None,
+                unit_flops * hidden * 2,
+            )
+            d_m, d_s, last = tensor_sum(mine, send)
+            kept[t] = (dy, d_m, d_s, sums_mlp)
+            pieces[0].append((g, dm))
+            pieces[1].append((records[ticks - 1 - t][6], du))
+        for t in group:
+            x, n1, qkv, o, a_m, a_s = records[ticks - 1 - t][:6]
+            dy, d_m, d_s, sums_mlp = kept[t]
+            dh, da, dqkv, mine, send, sums_attn, pair = call(
+                partial(attn_bwd_kernel, seq),
+                (flags, x, a_m, a_s, dy, d_m, d_s, qkv, vec, wqkv, wout),
+                [wide(rows, width), low(rows, width), low(rows, 3 * share)]
+                + halves
+                + [wide(4, width), wide(2, share)],
+                last,
+                flops=unit_flops * share * 10,
+            )
+            d_m, d_s, last = tensor_sum(mine, send)
+            kept[t] = (dh, d_m, d_s, sums_mlp, sums_attn, pair)
+            pieces[2].append((o, da))
+            pieces[3].append((n1, dqkv))
+        for t in group:
+            dh, d_m, d_s, sums_mlp, sums_attn, pair = kept[t]
+            dx, half, sums_in = call(
+                in_bwd_kernel,
+                (flags, records[ticks - 1 - t][0], dh, d_m, d_s, vec),
+                [wide(seq, width), low(rows, width // 2), wide(2, width)],
+                last,
+            )
+            grads.append(dx)
+            if t + LAG < ticks:
+                returns[t + LAG] = passed_along(half, -1)
+            small.append((sums_mlp, sums_attn, sums_in, pair))
+
+    def grad_of(piece, blocks, after):
+        return weight_grad([p[0] for p in piece], [p[1] for p in piece], blocks, after)
+
+    grad_fc2 = grad_of(pieces[0], 2, last)
+    grad_fc1 = grad_of(pieces[1], 2, last)
+    grad_fc2, grad_fc1 = lax.psum((grad_fc2, grad_fc1), "dp")
+    grad_out = grad_of(pieces[2], 2, last)
+    grad_qkv = grad_of(pieces[3], 3, last)
     sums_mlp, sums_attn, sums_in, pair = [sum(s[1:], s[0]) for s in zip(*small)]
-    grad_vec = jnp.concatenate([sums_in, sums_attn[2:4], sums_attn[0:2], sums_mlp[0:2]], axis=0)
-    summed = lax.psum(
-        (
-            grad_fc2,
-            grad_fc1,
-            grad_qkv,
-            grad_out,
-            grad_vec.astype(LOW),
-            sums_mlp[2:3].astype(LOW),
-            pair.astype(LOW),
-        ),
-        "dp",
+    rest = pair.size
+    tail_rows = 9 + -(-rest // width)
+    tail = jnp.concatenate(
+        [
+            sums_in,
+            sums_attn[2:4],
+            sums_attn[0:2],
+            sums_mlp,
+            jnp.pad(pair.reshape(-1), (0, (tail_rows - 9) * width - rest)).reshape(-1, width),
+        ],
+        axis=0,
     )
-    grad_fc2, grad_fc1, grad_qkv, grad_out, grad_vec, grad_fc1b, grad_pair = [
-        s.astype(F32) for s in summed
+    tail_rows = -(-tail_rows // 16) * 16
+    tail = jnp.pad(tail, ((0, tail_rows - tail.shape[0]), (0, 0))).astype(LOW)
+    grad_out = jnp.concatenate([grad_out, tail.reshape(tail_rows, 2, -1).swapaxes(0, 1)], axis=1)
+    grad_out, grad_qkv = lax.psum(
+        tuple(held_until(held_until(g, grad_fc1), grad_fc2) for g in (grad_out, grad_qkv)), "dp"
+    )
+    tail = grad_out[:, share:].swapaxes(0, 1).reshape(tail_rows, width).astype(F32)
+    grad_out = grad_out[:, :share]
+    grad_vec, grad_fc1b = tail[0:8], tail[8:9]
+    grad_pair = tail[9:].reshape(-1)[:rest].reshape(pair.shape)
+    grad_fc2, grad_fc1, grad_qkv, grad_out = [
+        g.astype(F32) for g in (grad_fc2, grad_fc1, grad_qkv, grad_out)
     ]
 
     def columns(blocked):
@@ -375,7 +450,7 @@
 
     shape_out = (1, micro_count, images, seq, width)
     outputs = jnp.stack(
-        [jnp.where(first, results[m][0, :seq], results[m + LAG][0, :seq]) for m in range(units)]
+        [jnp.where(first, results[m][:seq], results[m + LAG][:seq]) for m in range(units)]
     ).reshape(shape_out)
     input_grads = jnp.stack(
         [jnp.where(first, grads[ticks - 1 - m], grads[units - 1 - m]) for m in range(units)]

time: 1030 us -> 848 us (0.82)
  waiting for transfers between devices: 519 us -> 361 us
  blocking collectives: 21.3 us -> 0 us
  local copies, waits for them, and re-layouts: 105 us -> 93.8 us
    ppermute x16, waiting for transfers between devices: 149 us -> 67.3 us  [passed_along(): arrived = lax.ppermute(block, 'section', route)]
    ppermute x120 -> x136, waiting for transfers between devices: 224 us -> 145 us  [swap(): return lax.ppermute(value, 'tensor', route)]
    psum x1 -> x0, blocking collectives: 21.3 us -> none  [body(): lax.psum((grad_fc2, grad_fc1, grad_qkv, grad_out, grad_vec.astype(LOW), s...]
    unnamed x794 -> x817, local copies, waits for them, and re-layouts: 100 us -> 86.8 us
    ppermute x16, starting transfers between devices: 33.3 us -> 45.8 us  [passed_along(): arrived = lax.ppermute(block, 'section', route)]
    ppermute x120 -> x136, starting transfers between devices: 71.6 us -> 60 us  [swap(): return lax.ppermute(value, 'tensor', route)]
    pallas_call x60 -> x64, Pallas kernels: 176 us -> 179 us  [the longest x60 179 us: call(): pl.pallas_call(partial(skip_last, kernel, len(args)), grid=(1,), in_specs...]
    psum x1 -> x2, waiting for transfers between devices: 146 us -> 149 us  [the longest x1 88.2 us: body(): grad_fc2, grad_fc1 = lax.psum((grad_fc2, grad_fc1), 'dp')]
  transfers between devices with their start and end apart: 137 -> 154, of which waited for: 55 -> 95; matrix products, arithmetic and copies ran while one was open for 4% -> 7% of each run, Pallas kernels for 19% -> 22%
where the time goes in v2:
time: 848 us; the launch traced here: 833 us
  waiting for transfers between devices  361 us (43%)
  Pallas kernels  215 us (25%)
  starting transfers between devices  106 us (12%)
  local copies, waits for them, and re-layouts  93.8 us (11%)
  other arithmetic  36 us (4%)
  between operations  20.4 us (2%)
    pallas_call x60, Pallas kernels, call(): pl.pallas_call(partial(skip_last, kernel, len(args)), grid=(1,), in_specs...  179 us
    ppermute x136, waiting for transfers between devices, swap(): return lax.ppermute(value, 'tensor', route)  145 us
    psum x1, waiting for transfers between devices, body(): grad_fc2, grad_fc1 = lax.psum((grad_fc2, grad_fc1), 'dp')  88.2 us
    unnamed x817, local copies, waits for them, and re-layouts  86.8 us
    ppermute x16, waiting for transfers between devices, passed_along(): arrived = lax.ppermute(block, 'section', route)  67.3 us
    psum x1, waiting for transfers between devices, body(): lax.psum(tuple((held_until(held_until(g, grad_fc1), grad_fc2) for g in (g...  60.7 us
    ppermute x136, starting transfers between devices, swap(): return lax.ppermute(value, 'tensor', route)  60 us
    ppermute x16, starting transfers between devices, passed_along(): arrived = lax.ppermute(block, 'section', route)  45.8 us
  transfers between devices with their start and end apart: 154, of which 95 were waited for; matrix products, arithmetic and copies ran while one was open for 7% of the time, Pallas kernels for 22%

profile of v2, /device:TPU:0, one launch (start us, length us, event | category | flops | bytes accessed | tf_op | source)
XLA Modules:
  0.0 832.6 jit_solution(14975992806002980169)
XLA Ops:
  8.6 5.6 copy.26
  30.3 3.5 collective-permute-done.1
  39.4 3.8 collective-permute-done.7
  56.0 3.4 collective-permute-start.10
  67.6 4.4 collective-permute-start.17
  83.7 4.1 collective-permute-done.13
  92.9 4.3 collective-permute-done.23
  109.3 4.4 collective-permute-start.28
  116.0 3.8 collective-permute-done.28.refs_2_
  121.0 4.6 collective-permute-start.33
  125.5 3.3 shard_map.172
  137.1 4.1 collective-permute-done.31
  146.2 4.3 collective-permute-done.39
  162.6 4.4 collective-permute-start.44
  169.4 3.8 collective-permute-done.44.refs_2_
  174.3 4.6 collective-permute-start.49
  178.9 3.3 shard_map.178
  190.4 4.1 collective-permute-done.47
  199.6 4.3 collective-permute-done.55
  209.6 3.6 collective-permute-done.53
  216.0 4.4 collective-permute-start.60
  222.8 3.8 collective-permute-done.60.refs_2_
  227.7 4.8 collective-permute-start.65
  243.7 4.1 collective-permute-done.63
  252.9 4.3 collective-permute-done.71
  264.8 7.8 collective-permute-done.74
  273.7 3.5 copy.27
  286.7 4.8 collective-permute-done.80
  293.2 5.8 shard_map.192
  302.5 6.2 shard_map.193
  315.9 3.7 collective-permute-done.84
  319.7 5.6 collective-permute-done.90.refs_2_
  332.8 5.6 collective-permute-done.86.refs_2_
  343.0 4.6 collective-permute-done.96
  349.4 5.8 shard_map.198
  358.7 5.9 shard_map.199
  372.0 3.7 collective-permute-done.100
  375.8 5.4 collective-permute-done.106.refs_2_
  388.3 5.5 collective-permute-done.102.refs_2_
  398.4 4.6 collective-permute-done.112
  404.8 5.8 shard_map.204
  414.1 6.2 shard_map.205
  427.4 3.7 collective-permute-done.116
  431.3 5.5 collective-permute-done.122.refs_2_
  444.3 5.5 collective-permute-done.118.refs_2_
  454.4 4.6 collective-permute-done.128
  460.8 5.8 shard_map.210
  470.2 5.9 shard_map.211
  483.5 3.6 collective-permute-done.132
  487.3 5.5 collective-permute-done.138.refs_2_
  499.1 6.2 collective-permute-done.134.refs_2_
  510.1 4.4 collective-permute-done.144
  516.3 5.8 shard_map.216
  526.4 6.0 shard_map.217
  543.1 11.7 %shard_map.223 = bf16[2,1024,512]{2,1,0:T(8,128)(2,1)S(1)} custom-call(bf16[272,1024]{1,0:T(8,128)(2,1)S(1)} %copy-done.399, bf16[272,1024]{1,0:T(8,128)(2,1)S(1)} %copy-done.395, bf16[272,1024]{1,0:T(8,128)(2,1)S(1)} %copy-done.391, bf16[272,1024]{1,0:T(8,128)(2,1)S(1)} %copy-done.387, bf16[272,1024]{1,0:T(8,128)(2,1)S(1)} %copy-done.383, ...), custom_call_target="tpu_custom_call" | custom-call | flops 5704253440 | bytes 13238272 | tf_op jit(solution)/shard_map/pallas_call | solution.py:244
  559.5 11.7 %shard_map.221 = bf16[2,1024,512]{2,1,0:T(8,128)(2,1)S(1)} custom-call(bf16[272,1024]{1,0:T(8,128)(2,1)S(1)} %copy-done.397, bf16[272,1024]{1,0:T(8,128)(2,1)S(1)} %copy-done.393, bf16[272,1024]{1,0:T(8,128)(2,1)S(1)} %copy-done.389, bf16[272,1024]{1,0:T(8,128)(2,1)S(1)} %copy-done.385, bf16[272,1024]{1,0:T(8,128)(2,1)S(1)} %copy-done.381, ...), custom_call_target="tpu_custom_call" | custom-call | flops 5704253440 | bytes 13238272 | tf_op jit(solution)/shard_map/pallas_call | solution.py:244
  583.2 8.7 %copy.30 = bf16[1,4,2,257,1024]{4,2,3,1,0:T(2,128)(2,1)} copy(bf16[1,4,2,257,1024]{4,3,2,1,0:T(8,128)(2,1)} %bitcast.164) | data formatting | bytes 8421376
  595.0 7.1 collective-permute-done.150
  611.0 3.7 shard_map.220
  617.8 9.2 %shard_map.225.value = bf16[3,1024,256]{2,1,0:T(8,128)(2,1)S(1)} custom-call(bf16[272,1024]{1,0:T(8,128)(2,1)S(1)} %copy-done.359, bf16[272,1024]{1,0:T(8,128)(2,1)S(1)} %copy-done.357, bf16[272,1024]{1,0:T(8,128)(2,1)S(1)} %copy-done.281, bf16[272,1024]{1,0:T(8,128)(2,1)S(1)} %copy-done.279, bf16[272,1024]{1,0:T(8,128)(2,1)S(1)} %copy-done.277, ...), custom_call_target="tpu_custom_call" | custom-call | flops 4278190080 | bytes 11321344 | tf_op jit(solution)/shard_map/pallas_call | solution.py:244
  639.8 88.2 %all-reduce.11.cloned.1.call-done = (bf16[2,1024,512]{2,1,0:T(8,128)(2,1)}, bf16[2,1024,512]{2,1,0:T(8,128)(2,1)}) async-done(((bf16[2,1024,512]{2,1,0:T(8,128)(2,1)}, bf16[2,1024,512]{2,1,0:T(8,128)(2,1)}), (bf16[2,1024,512]{2,1,0:T(8,128)(2,1)}, bf16[2,1024,512]{2,1,0:T(8,128)(2,1)})) %all-reduce.11.cloned.1.call-update) | async-done | bytes 4194320 | tf_op jit(solution)/shard_map/psum | solution.py:418
  734.3 15.8 %copy.31 = f32[1,4,2,257,1024]{4,2,3,1,0:T(2,128)} copy(f32[1,4,2,257,1024]{4,3,2,1,0:T(8,128)} %bitcast.29) | data formatting | bytes 16842752
  753.2 4.6 maximum_bitcast_fusion
  757.8 60.7 %all-reduce.9.cloned.1.call-done = (bf16[2,272,512]{2,1,0:T(8,128)(2,1)}, bf16[1,3,1024,256]{3,2,1,0:T(8,128)(2,1)}) async-done(((bf16[2,272,512]{2,1,0:T(8,128)(2,1)}, bf16[1,3,1024,256]{3,2,1,0:T(8,128)(2,1)}), (bf16[2,272,512]{2,1,0:T(8,128)(2,1)}, bf16[1,3,1024,256]{3,2,1,0:T(8,128)(2,1)})) %all-reduce.9.cloned.1.call-update) | async-done | bytes 2129936 | tf_op jit(solution)/shard_map/psum | solution.py:437
  (1262 shorter events, 334.6 us)
Async XLA Ops:
  7.2 720.8 %all-reduce.11.cloned.1.call-start = ((), (), s32[]{:S(2)}) async-start(), calls=%async_computation.1 | async-start | bytes 8388608 | tf_op jit(solution)/shard_map/psum | solution.py:418
  23.9 9.9 %collective-permute-start.1 = (bf16[272,512]{1,0:T(8,128)(2,1)S(1)}, bf16[272,512]{1,0:T(8,128)(2,1)S(1)}, u32[]{:S(2)}, u32[]{:S(2)}) collective-permute-start(bf16[272,512]{1,0:T(8,128)(2,1)S(1)} %add_convert_fusion.79.refs_8_), channel_id=1, source_target_pairs={{0,8},{4,12},{8,0},{12,4},{1,9},{5,13},{9,1},{13,5},{2,10},{6,14},... | collective-permute-start | bytes 835592 | tf_op jit(solution)/shard_map/ppermute | solution.py:277
  34.1 9.1 %collective-permute-start.7 = (bf16[272,512]{1,0:T(8,128)(2,1)S(1)}, bf16[272,512]{1,0:T(8,128)(2,1)S(1)}, u32[]{:S(2)}, u32[]{:S(2)}) collective-permute-start(bf16[272,512]{1,0:T(8,128)(2,1)S(1)} %add_convert_fusion.77.refs_8_), channel_id=1, source_target_pairs={{0,8},{4,12},{8,0},{12,4},{1,9},{5,13},{9,1},{13,5},{2,10},{6,14},... | collective-permute-start | bytes 835592 | tf_op jit(solution)/shard_map/ppermute | solution.py:277
  43.4 9.1 %collective-permute-start.5 = (bf16[272,512]{1,0:T(8,128)(2,1)S(1)}, bf16[272,512]{1,0:T(8,128)(2,1)S(1)}, u32[]{:S(2)}, u32[]{:S(2)}) collective-permute-start(bf16[272,512]{1,0:T(8,128)(2,1)S(1)} %add_convert_fusion.76.refs_8_), channel_id=1, source_target_pairs={{0,8},{4,12},{8,0},{12,4},{1,9},{5,13},{9,1},{13,5},{2,10},{6,14},... | collective-permute-start | bytes 835592 | tf_op jit(solution)/shard_map/ppermute | solution.py:277
  53.2 9.1 %collective-permute-start.15 = (bf16[272,512]{1,0:T(8,128)(2,1)S(1)}, bf16[272,512]{1,0:T(8,128)(2,1)S(1)}, u32[]{:S(2)}, u32[]{:S(2)}) collective-permute-start(bf16[272,512]{1,0:T(8,128)(2,1)S(1)} %add_convert_fusion.73.refs_7_.refs_8_), channel_id=1, source_target_pairs={{0,8},{4,12},{8,0},{12,4},{1,9},{5,13},{9,1},{13,5},{2,10},{6,14},... | collective-permute-start | bytes 835592 | tf_op jit(solution)/shard_map/ppermute | solution.py:277
  56.0 9.7 %collective-permute-start.10 = (bf16[272,512]{1,0:T(8,128)(2,1)S(1)}, bf16[272,512]{1,0:T(8,128)(2,1)S(1)}, u32[]{:S(2)}, u32[]{:S(2)}) collective-permute-start(bf16[272,512]{1,0:T(8,128)(2,1)S(1)} %get-tuple-element.306), channel_id=1, source_target_pairs={{0,16},{1,17},{2,18},{3,19},{4,20},{5,21},{6,22},{7,23},{8,24},{9,... | collective-permute-start | bytes 835592 | tf_op jit(solution)/shard_map/ppermute | solution.py:295
  65.7 6.3 collective-permute-start.11
  67.6 10.9 %collective-permute-start.17 = (bf16[272,512]{1,0:T(8,128)(2,1)S(1)}, bf16[272,512]{1,0:T(8,128)(2,1)S(1)}, u32[]{:S(2)}, u32[]{:S(2)}) collective-permute-start(bf16[272,512]{1,0:T(8,128)(2,1)S(1)} %get-tuple-element.310), channel_id=1, source_target_pairs={{0,16},{1,17},{2,18},{3,19},{4,20},{5,21},{6,22},{7,23},{8,24},{9,... | collective-permute-start | bytes 835592 | tf_op jit(solution)/shard_map/ppermute | solution.py:295
  78.6 9.1 %collective-permute-start.13 = (bf16[272,512]{1,0:T(8,128)(2,1)S(1)}, bf16[272,512]{1,0:T(8,128)(2,1)S(1)}, u32[]{:S(2)}, u32[]{:S(2)}) collective-permute-start(bf16[272,512]{1,0:T(8,128)(2,1)S(1)} %add_convert_fusion.72.refs_8_), channel_id=1, source_target_pairs={{0,8},{4,12},{8,0},{12,4},{1,9},{5,13},{9,1},{13,5},{2,10},{6,14},... | collective-permute-start | bytes 835592 | tf_op jit(solution)/shard_map/ppermute | solution.py:277
  88.0 9.1 %collective-permute-start.23 = (bf16[272,512]{1,0:T(8,128)(2,1)S(1)}, bf16[272,512]{1,0:T(8,128)(2,1)S(1)}, u32[]{:S(2)}, u32[]{:S(2)}) collective-permute-start(bf16[272,512]{1,0:T(8,128)(2,1)S(1)} %add_convert_fusion.69.refs_8_), channel_id=1, source_target_pairs={{0,8},{4,12},{8,0},{12,4},{1,9},{5,13},{9,1},{13,5},{2,10},{6,14},... | collective-permute-start | bytes 835592 | tf_op jit(solution)/shard_map/ppermute | solution.py:277
  97.4 9.1 %collective-permute-start.21 = (bf16[272,512]{1,0:T(8,128)(2,1)S(1)}, bf16[272,512]{1,0:T(8,128)(2,1)S(1)}, u32[]{:S(2)}, u32[]{:S(2)}) collective-permute-start(bf16[272,512]{1,0:T(8,128)(2,1)S(1)} %add_convert_fusion.68.refs_8_), channel_id=1, source_target_pairs={{0,8},{4,12},{8,0},{12,4},{1,9},{5,13},{9,1},{13,5},{2,10},{6,14},... | collective-permute-start | bytes 835592 | tf_op jit(solution)/shard_map/ppermute | solution.py:277
  106.8 9.1 %collective-permute-start.26 = (bf16[272,512]{1,0:T(8,128)(2,1)S(1)}, bf16[272,512]{1,0:T(8,128)(2,1)S(1)}, u32[]{:S(2)}, u32[]{:S(2)}) collective-permute-start(bf16[272,512]{1,0:T(8,128)(2,1)S(1)} %add_convert_fusion.65.refs_7_.refs_8_), channel_id=1, source_target_pairs={{0,8},{4,12},{8,0},{12,4},{1,9},{5,13},{9,1},{13,5},{2,10},{6,14},... | collective-permute-start | bytes 835592 | tf_op jit(solution)/shard_map/ppermute | solution.py:277
  109.3 10.6 %collective-permute-start.28 = (bf16[272,512]{1,0:T(8,128)(2,1)S(1)}, bf16[272,512]{1,0:T(8,128)(2,1)S(1)}, u32[]{:S(2)}, u32[]{:S(2)}) collective-permute-start(bf16[272,512]{1,0:T(8,128)(2,1)S(1)} %get-tuple-element.321), channel_id=1, source_target_pairs={{0,16},{1,17},{2,18},{3,19},{4,20},{5,21},{6,22},{7,23},{8,24},{9,... | collective-permute-start | bytes 835592 | tf_op jit(solution)/shard_map/ppermute | solution.py:295
  121.0 11.0 %collective-permute-start.33 = (bf16[272,512]{1,0:T(8,128)(2,1)S(1)}, bf16[272,512]{1,0:T(8,128)(2,1)S(1)}, u32[]{:S(2)}, u32[]{:S(2)}) collective-permute-start(bf16[272,512]{1,0:T(8,128)(2,1)S(1)} %get-tuple-element.325), channel_id=1, source_target_pairs={{0,16},{1,17},{2,18},{3,19},{4,20},{5,21},{6,22},{7,23},{8,24},{9,... | collective-permute-start | bytes 835592 | tf_op jit(solution)/shard_map/ppermute | solution.py:295
  132.0 9.1 %collective-permute-start.31 = (bf16[272,512]{1,0:T(8,128)(2,1)S(1)}, bf16[272,512]{1,0:T(8,128)(2,1)S(1)}, u32[]{:S(2)}, u32[]{:S(2)}) collective-permute-start(bf16[272,512]{1,0:T(8,128)(2,1)S(1)} %add_convert_fusion.63.refs_8_), channel_id=1, source_target_pairs={{0,8},{4,12},{8,0},{12,4},{1,9},{5,13},{9,1},{13,5},{2,10},{6,14},... | collective-permute-start | bytes 835592 | tf_op jit(solution)/shard_map/ppermute | solution.py:277
  141.4 9.1 %collective-permute-start.39 = (bf16[272,512]{1,0:T(8,128)(2,1)S(1)}, bf16[272,512]{1,0:T(8,128)(2,1)S(1)}, u32[]{:S(2)}, u32[]{:S(2)}) collective-permute-start(bf16[272,512]{1,0:T(8,128)(2,1)S(1)} %add_convert_fusion.61.refs_8_), channel_id=1, source_target_pairs={{0,8},{4,12},{8,0},{12,4},{1,9},{5,13},{9,1},{13,5},{2,10},{6,14},... | collective-permute-start | bytes 835592 | tf_op jit(solution)/shard_map/ppermute | solution.py:277
  150.8 9.1 %collective-permute-start.37 = (bf16[272,512]{1,0:T(8,128)(2,1)S(1)}, bf16[272,512]{1,0:T(8,128)(2,1)S(1)}, u32[]{:S(2)}, u32[]{:S(2)}) collective-permute-start(bf16[272,512]{1,0:T(8,128)(2,1)S(1)} %add_convert_fusion.60.refs_8_), channel_id=1, source_target_pairs={{0,8},{4,12},{8,0},{12,4},{1,9},{5,13},{9,1},{13,5},{2,10},{6,14},... | collective-permute-start | bytes 835592 | tf_op jit(solution)/shard_map/ppermute | solution.py:277
  160.1 9.1 %collective-permute-start.42 = (bf16[272,512]{1,0:T(8,128)(2,1)S(1)}, bf16[272,512]{1,0:T(8,128)(2,1)S(1)}, u32[]{:S(2)}, u32[]{:S(2)}) collective-permute-start(bf16[272,512]{1,0:T(8,128)(2,1)S(1)} %add_convert_fusion.57.refs_7_.refs_8_), channel_id=1, source_target_pairs={{0,8},{4,12},{8,0},{12,4},{1,9},{5,13},{9,1},{13,5},{2,10},{6,14},... | collective-permute-start | bytes 835592 | tf_op jit(solution)/shard_map/ppermute | solution.py:277
  162.6 10.6 %collective-permute-start.44 = (bf16[272,512]{1,0:T(8,128)(2,1)S(1)}, bf16[272,512]{1,0:T(8,128)(2,1)S(1)}, u32[]{:S(2)}, u32[]{:S(2)}) collective-permute-start(bf16[272,512]{1,0:T(8,128)(2,1)S(1)} %get-tuple-element.335), channel_id=1, source_target_pairs={{0,16},{1,17},{2,18},{3,19},{4,20},{5,21},{6,22},{7,23},{8,24},{9,... | collective-permute-start | bytes 835592 | tf_op jit(solution)/shard_map/ppermute | solution.py:295
  174.3 11.0 %collective-permute-start.49 = (bf16[272,512]{1,0:T(8,128)(2,1)S(1)}, bf16[272,512]{1,0:T(8,128)(2,1)S(1)}, u32[]{:S(2)}, u32[]{:S(2)}) collective-permute-start(bf16[272,512]{1,0:T(8,128)(2,1)S(1)} %get-tuple-element.339), channel_id=1, source_target_pairs={{0,16},{1,17},{2,18},{3,19},{4,20},{5,21},{6,22},{7,23},{8,24},{9,... | collective-permute-start | bytes 835592 | tf_op jit(solution)/shard_map/ppermute | solution.py:295
  185.4 9.1 %collective-permute-start.47 = (bf16[272,512]{1,0:T(8,128)(2,1)S(1)}, bf16[272,512]{1,0:T(8,128)(2,1)S(1)}, u32[]{:S(2)}, u32[]{:S(2)}) collective-permute-start(bf16[272,512]{1,0:T(8,128)(2,1)S(1)} %add_convert_fusion.55.refs_8_), channel_id=1, source_target_pairs={{0,8},{4,12},{8,0},{12,4},{1,9},{5,13},{9,1},{13,5},{2,10},{6,14},... | collective-permute-start | bytes 835592 | tf_op jit(solution)/shard_map/ppermute | solution.py:277
  194.7 9.1 %collective-permute-start.55 = (bf16[272,512]{1,0:T(8,128)(2,1)S(1)}, bf16[272,512]{1,0:T(8,128)(2,1)S(1)}, u32[]{:S(2)}, u32[]{:S(2)}) collective-permute-start(bf16[272,512]{1,0:T(8,128)(2,1)S(1)} %add_convert_fusion.53.refs_8_), channel_id=1, source_target_pairs={{0,8},{4,12},{8,0},{12,4},{1,9},{5,13},{9,1},{13,5},{2,10},{6,14},... | collective-permute-start | bytes 835592 | tf_op jit(solution)/shard_map/ppermute | solution.py:277
  204.1 9.1 %collective-permute-start.53 = (bf16[272,512]{1,0:T(8,128)(2,1)S(1)}, bf16[272,512]{1,0:T(8,128)(2,1)S(1)}, u32[]{:S(2)}, u32[]{:S(2)}) collective-permute-start(bf16[272,512]{1,0:T(8,128)(2,1)S(1)} %add_convert_fusion.52.refs_8_), channel_id=1, source_target_pairs={{0,8},{4,12},{8,0},{12,4},{1,9},{5,13},{9,1},{13,5},{2,10},{6,14},... | collective-permute-start | bytes 835592 | tf_op jit(solution)/shard_map/ppermute | solution.py:277
  213.5 9.1 %collective-permute-start.58 = (bf16[272,512]{1,0:T(8,128)(2,1)S(1)}, bf16[272,512]{1,0:T(8,128)(2,1)S(1)}, u32[]{:S(2)}, u32[]{:S(2)}) collective-permute-start(bf16[272,512]{1,0:T(8,128)(2,1)S(1)} %add_convert_fusion.49.refs_7_.refs_8_), channel_id=1, source_target_pairs={{0,8},{4,12},{8,0},{12,4},{1,9},{5,13},{9,1},{13,5},{2,10},{6,14},... | collective-permute-start | bytes 835592 | tf_op jit(solution)/shard_map/ppermute | solution.py:277
  216.0 10.6 %collective-permute-start.60 = (bf16[272,512]{1,0:T(8,128)(2,1)S(1)}, bf16[272,512]{1,0:T(8,128)(2,1)S(1)}, u32[]{:S(2)}, u32[]{:S(2)}) collective-permute-start(bf16[272,512]{1,0:T(8,128)(2,1)S(1)} %get-tuple-element.349), channel_id=1, source_target_pairs={{0,16},{1,17},{2,18},{3,19},{4,20},{5,21},{6,22},{7,23},{8,24},{9,... | collective-permute-start | bytes 835592 | tf_op jit(solution)/shard_map/ppermute | solution.py:295
  227.7 11.0 %collective-permute-start.65 = (bf16[272,512]{1,0:T(8,128)(2,1)S(1)}, bf16[272,512]{1,0:T(8,128)(2,1)S(1)}, u32[]{:S(2)}, u32[]{:S(2)}) collective-permute-start(bf16[272,512]{1,0:T(8,128)(2,1)S(1)} %get-tuple-element.353), channel_id=1, source_target_pairs={{0,16},{1,17},{2,18},{3,19},{4,20},{5,21},{6,22},{7,23},{8,24},{9,... | collective-permute-start | bytes 835592 | tf_op jit(solution)/shard_map/ppermute | solution.py:295
  238.7 9.1 %collective-permute-start.63 = (bf16[272,512]{1,0:T(8,128)(2,1)S(1)}, bf16[272,512]{1,0:T(8,128)(2,1)S(1)}, u32[]{:S(2)}, u32[]{:S(2)}) collective-permute-start(bf16[272,512]{1,0:T(8,128)(2,1)S(1)} %add_convert_fusion.47.refs_8_), channel_id=1, source_target_pairs={{0,8},{4,12},{8,0},{12,4},{1,9},{5,13},{9,1},{13,5},{2,10},{6,14},... | collective-permute-start | bytes 835592 | tf_op jit(solution)/shard_map/ppermute | solution.py:277
  248.1 9.1 %collective-permute-start.71 = (bf16[272,512]{1,0:T(8,128)(2,1)S(1)}, bf16[272,512]{1,0:T(8,128)(2,1)S(1)}, u32[]{:S(2)}, u32[]{:S(2)}) collective-permute-start(bf16[272,512]{1,0:T(8,128)(2,1)S(1)} %add_convert_fusion.45.refs_8_), channel_id=1, source_target_pairs={{0,8},{4,12},{8,0},{12,4},{1,9},{5,13},{9,1},{13,5},{2,10},{6,14},... | collective-permute-start | bytes 835592 | tf_op jit(solution)/shard_map/ppermute | solution.py:277
  263.8 8.8 %collective-permute-start.74 = (bf16[272,512]{1,0:T(8,128)(2,1)S(1)}, bf16[272,512]{1,0:T(8,128)(2,1)S(1)}, u32[]{:S(2)}, u32[]{:S(2)}) collective-permute-start(bf16[272,512]{1,0:T(8,128)(2,1)S(1)} %add_convert_fusion.41.refs_7_.refs_10_), channel_id=1, source_target_pairs={{0,8},{4,12},{8,0},{12,4},{1,9},{5,13},{9,1},{13,5},{2,10},{6,14},... | collective-permute-start | bytes 835592 | tf_op jit(solution)/shard_map/ppermute | solution.py:277
  272.7 9.1 %collective-permute-start.69 = (bf16[272,512]{1,0:T(8,128)(2,1)S(1)}, bf16[272,512]{1,0:T(8,128)(2,1)S(1)}, u32[]{:S(2)}, u32[]{:S(2)}) collective-permute-start(bf16[272,512]{1,0:T(8,128)(2,1)S(1)} %add_convert_fusion.44.refs_8_), channel_id=1, source_target_pairs={{0,8},{4,12},{8,0},{12,4},{1,9},{5,13},{9,1},{13,5},{2,10},{6,14},... | collective-permute-start | bytes 835592 | tf_op jit(solution)/shard_map/ppermute | solution.py:277
  282.7 8.8 %collective-permute-start.80 = (bf16[272,512]{1,0:T(8,128)(2,1)S(1)}, bf16[272,512]{1,0:T(8,128)(2,1)S(1)}, u32[]{:S(2)}, u32[]{:S(2)}) collective-permute-start(bf16[272,512]{1,0:T(8,128)(2,1)S(1)} %add_convert_fusion.39.refs_10_), channel_id=1, source_target_pairs={{0,8},{4,12},{8,0},{12,4},{1,9},{5,13},{9,1},{13,5},{2,10},{6,14},... | collective-permute-start | bytes 835592 | tf_op jit(solution)/shard_map/ppermute | solution.py:277
  291.7 9.1 %collective-permute-start.78 = (bf16[272,512]{1,0:T(8,128)(2,1)S(1)}, bf16[272,512]{1,0:T(8,128)(2,1)S(1)}, u32[]{:S(2)}, u32[]{:S(2)}) collective-permute-start(bf16[272,512]{1,0:T(8,128)(2,1)S(1)} %add_convert_fusion.38.refs_11_), channel_id=1, source_target_pairs={{0,8},{4,12},{8,0},{12,4},{1,9},{5,13},{9,1},{13,5},{2,10},{6,14},... | collective-permute-start | bytes 835592 | tf_op jit(solution)/shard_map/ppermute | solution.py:277
  301.1 9.1 %collective-permute-start.88 = (bf16[272,512]{1,0:T(8,128)(2,1)S(1)}, bf16[272,512]{1,0:T(8,128)(2,1)S(1)}, u32[]{:S(2)}, u32[]{:S(2)}) collective-permute-start(bf16[272,512]{1,0:T(8,128)(2,1)S(1)} %add_convert_fusion.35.refs_11_), channel_id=1, source_target_pairs={{0,8},{4,12},{8,0},{12,4},{1,9},{5,13},{9,1},{13,5},{2,10},{6,14},... | collective-permute-start | bytes 835592 | tf_op jit(solution)/shard_map/ppermute | solution.py:277
  310.5 9.1 %collective-permute-start.84 = (bf16[272,512]{1,0:T(8,128)(2,1)S(1)}, bf16[272,512]{1,0:T(8,128)(2,1)S(1)}, u32[]{:S(2)}, u32[]{:S(2)}) collective-permute-start(bf16[272,512]{1,0:T(8,128)(2,1)S(1)} %add_convert_fusion.34.refs_6_.refs_10_), channel_id=1, source_target_pairs={{0,8},{4,12},{8,0},{12,4},{1,9},{5,13},{9,1},{13,5},{2,10},{6,14},... | collective-permute-start | bytes 835592 | tf_op jit(solution)/shard_map/ppermute | solution.py:277
  314.5 10.8 %collective-permute-start.90 = (bf16[272,512]{1,0:T(8,128)(2,1)S(1)}, bf16[272,512]{1,0:T(8,128)(2,1)S(1)}, u32[]{:S(2)}, u32[]{:S(2)}) collective-permute-start(bf16[272,512]{1,0:T(8,128)(2,1)S(1)} %get-tuple-element.381), channel_id=1, source_target_pairs={{16,0},{17,1},{18,2},{19,3},{20,4},{21,5},{22,6},{23,7},{24,8},{25... | collective-permute-start | bytes 835592 | tf_op jit(solution)/shard_map/ppermute | solution.py:295
  327.4 10.9 %collective-permute-start.86 = (bf16[272,512]{1,0:T(8,128)(2,1)S(1)}, bf16[272,512]{1,0:T(8,128)(2,1)S(1)}, u32[]{:S(2)}, u32[]{:S(2)}) collective-permute-start(bf16[272,512]{1,0:T(8,128)(2,1)S(1)} %get-tuple-element.378), channel_id=1, source_target_pairs={{16,0},{17,1},{18,2},{19,3},{20,4},{21,5},{22,6},{23,7},{24,8},{25... | collective-permute-start | bytes 835592 | tf_op jit(solution)/shard_map/ppermute | solution.py:295
  332.3 6.1 collective-permute-start.92
  338.5 9.1 %collective-permute-start.96 = (bf16[272,512]{1,0:T(8,128)(2,1)S(1)}, bf16[272,512]{1,0:T(8,128)(2,1)S(1)}, u32[]{:S(2)}, u32[]{:S(2)}) collective-permute-start(bf16[272,512]{1,0:T(8,128)(2,1)S(1)} %add_convert_fusion.31.refs_10_), channel_id=1, source_target_pairs={{0,8},{4,12},{8,0},{12,4},{1,9},{5,13},{9,1},{13,5},{2,10},{6,14},... | collective-permute-start | bytes 835592 | tf_op jit(solution)/shard_map/ppermute | solution.py:277
  347.8 9.1 %collective-permute-start.94 = (bf16[272,512]{1,0:T(8,128)(2,1)S(1)}, bf16[272,512]{1,0:T(8,128)(2,1)S(1)}, u32[]{:S(2)}, u32[]{:S(2)}) collective-permute-start(bf16[272,512]{1,0:T(8,128)(2,1)S(1)} %add_convert_fusion.30.refs_11_), channel_id=1, source_target_pairs={{0,8},{4,12},{8,0},{12,4},{1,9},{5,13},{9,1},{13,5},{2,10},{6,14},... | collective-permute-start | bytes 835592 | tf_op jit(solution)/shard_map/ppermute | solution.py:277
  357.2 9.1 %collective-permute-start.104 = (bf16[272,512]{1,0:T(8,128)(2,1)S(1)}, bf16[272,512]{1,0:T(8,128)(2,1)S(1)}, u32[]{:S(2)}, u32[]{:S(2)}) collective-permute-start(bf16[272,512]{1,0:T(8,128)(2,1)S(1)} %add_convert_fusion.27.refs_11_), channel_id=1, source_target_pairs={{0,8},{4,12},{8,0},{12,4},{1,9},{5,13},{9,1},{13,5},{2,10},{6,14},... | collective-permute-start | bytes 835592 | tf_op jit(solution)/shard_map/ppermute | solution.py:277
  366.6 9.1 %collective-permute-start.100 = (bf16[272,512]{1,0:T(8,128)(2,1)S(1)}, bf16[272,512]{1,0:T(8,128)(2,1)S(1)}, u32[]{:S(2)}, u32[]{:S(2)}) collective-permute-start(bf16[272,512]{1,0:T(8,128)(2,1)S(1)} %add_convert_fusion.26.refs_6_.refs_10_), channel_id=1, source_target_pairs={{0,8},{4,12},{8,0},{12,4},{1,9},{5,13},{9,1},{13,5},{2,10},{6,14},... | collective-permute-start | bytes 835592 | tf_op jit(solution)/shard_map/ppermute | solution.py:277
  370.6 10.7 %collective-permute-start.106 = (bf16[272,512]{1,0:T(8,128)(2,1)S(1)}, bf16[272,512]{1,0:T(8,128)(2,1)S(1)}, u32[]{:S(2)}, u32[]{:S(2)}) collective-permute-start(bf16[272,512]{1,0:T(8,128)(2,1)S(1)} %get-tuple-element.399), channel_id=1, source_target_pairs={{16,0},{17,1},{18,2},{19,3},{20,4},{21,5},{22,6},{23,7},{24,8},{25... | collective-permute-start | bytes 835592 | tf_op jit(solution)/shard_map/ppermute | solution.py:295
  382.8 11.0 %collective-permute-start.102 = (bf16[272,512]{1,0:T(8,128)(2,1)S(1)}, bf16[272,512]{1,0:T(8,128)(2,1)S(1)}, u32[]{:S(2)}, u32[]{:S(2)}) collective-permute-start(bf16[272,512]{1,0:T(8,128)(2,1)S(1)} %get-tuple-element.396), channel_id=1, source_target_pairs={{16,0},{17,1},{18,2},{19,3},{20,4},{21,5},{22,6},{23,7},{24,8},{25... | collective-permute-start | bytes 835592 | tf_op jit(solution)/shard_map/ppermute | solution.py:295
  393.9 9.1 %collective-permute-start.112 = (bf16[272,512]{1,0:T(8,128)(2,1)S(1)}, bf16[272,512]{1,0:T(8,128)(2,1)S(1)}, u32[]{:S(2)}, u32[]{:S(2)}) collective-permute-start(bf16[272,512]{1,0:T(8,128)(2,1)S(1)} %add_convert_fusion.23.refs_10_), channel_id=1, source_target_pairs={{0,8},{4,12},{8,0},{12,4},{1,9},{5,13},{9,1},{13,5},{2,10},{6,14},... | collective-permute-start | bytes 835592 | tf_op jit(solution)/shard_map/ppermute | solution.py:277
  403.3 9.1 %collective-permute-start.110 = (bf16[272,512]{1,0:T(8,128)(2,1)S(1)}, bf16[272,512]{1,0:T(8,128)(2,1)S(1)}, u32[]{:S(2)}, u32[]{:S(2)}) collective-permute-start(bf16[272,512]{1,0:T(8,128)(2,1)S(1)} %add_convert_fusion.22.refs_11_), channel_id=1, source_target_pairs={{0,8},{4,12},{8,0},{12,4},{1,9},{5,13},{9,1},{13,5},{2,10},{6,14},... | collective-permute-start | bytes 835592 | tf_op jit(solution)/shard_map/ppermute | solution.py:277
  412.6 9.1 %collective-permute-start.120 = (bf16[272,512]{1,0:T(8,128)(2,1)S(1)}, bf16[272,512]{1,0:T(8,128)(2,1)S(1)}, u32[]{:S(2)}, u32[]{:S(2)}) collective-permute-start(bf16[272,512]{1,0:T(8,128)(2,1)S(1)} %add_convert_fusion.19.refs_11_), channel_id=1, source_target_pairs={{0,8},{4,12},{8,0},{12,4},{1,9},{5,13},{9,1},{13,5},{2,10},{6,14},... | collective-permute-start | bytes 835592 | tf_op jit(solution)/shard_map/ppermute | solution.py:277
  422.1 9.1 %collective-permute-start.116 = (bf16[272,512]{1,0:T(8,128)(2,1)S(1)}, bf16[272,512]{1,0:T(8,128)(2,1)S(1)}, u32[]{:S(2)}, u32[]{:S(2)}) collective-permute-start(bf16[272,512]{1,0:T(8,128)(2,1)S(1)} %add_convert_fusion.18.refs_6_.refs_10_), channel_id=1, source_target_pairs={{0,8},{4,12},{8,0},{12,4},{1,9},{5,13},{9,1},{13,5},{2,10},{6,14},... | collective-permute-start | bytes 835592 | tf_op jit(solution)/shard_map/ppermute | solution.py:277
  426.0 10.7 %collective-permute-start.122 = (bf16[272,512]{1,0:T(8,128)(2,1)S(1)}, bf16[272,512]{1,0:T(8,128)(2,1)S(1)}, u32[]{:S(2)}, u32[]{:S(2)}) collective-permute-start(bf16[272,512]{1,0:T(8,128)(2,1)S(1)} %get-tuple-element.417), channel_id=1, source_target_pairs={{16,0},{17,1},{18,2},{19,3},{20,4},{21,5},{22,6},{23,7},{24,8},{25... | collective-permute-start | bytes 835592 | tf_op jit(solution)/shard_map/ppermute | solution.py:295
  438.9 10.9 %collective-permute-start.118 = (bf16[272,512]{1,0:T(8,128)(2,1)S(1)}, bf16[272,512]{1,0:T(8,128)(2,1)S(1)}, u32[]{:S(2)}, u32[]{:S(2)}) collective-permute-start(bf16[272,512]{1,0:T(8,128)(2,1)S(1)} %get-tuple-element.414), channel_id=1, source_target_pairs={{16,0},{17,1},{18,2},{19,3},{20,4},{21,5},{22,6},{23,7},{24,8},{25... | collective-permute-start | bytes 835592 | tf_op jit(solution)/shard_map/ppermute | solution.py:295
  443.8 6.1 collective-permute-start.124
  449.9 9.1 %collective-permute-start.128 = (bf16[272,512]{1,0:T(8,128)(2,1)S(1)}, bf16[272,512]{1,0:T(8,128)(2,1)S(1)}, u32[]{:S(2)}, u32[]{:S(2)}) collective-permute-start(bf16[272,512]{1,0:T(8,128)(2,1)S(1)} %add_convert_fusion.15.refs_10_), channel_id=1, source_target_pairs={{0,8},{4,12},{8,0},{12,4},{1,9},{5,13},{9,1},{13,5},{2,10},{6,14},... | collective-permute-start | bytes 835592 | tf_op jit(solution)/shard_map/ppermute | solution.py:277
  459.3 9.1 %collective-permute-start.126 = (bf16[272,512]{1,0:T(8,128)(2,1)S(1)}, bf16[272,512]{1,0:T(8,128)(2,1)S(1)}, u32[]{:S(2)}, u32[]{:S(2)}) collective-permute-start(bf16[272,512]{1,0:T(8,128)(2,1)S(1)} %add_convert_fusion.14.refs_11_), channel_id=1, source_target_pairs={{0,8},{4,12},{8,0},{12,4},{1,9},{5,13},{9,1},{13,5},{2,10},{6,14},... | collective-permute-start | bytes 835592 | tf_op jit(solution)/shard_map/ppermute | solution.py:277
  469.0 8.8 %collective-permute-start.136 = (bf16[272,512]{1,0:T(8,128)(2,1)S(1)}, bf16[272,512]{1,0:T(8,128)(2,1)S(1)}, u32[]{:S(2)}, u32[]{:S(2)}) collective-permute-start(bf16[272,512]{1,0:T(8,128)(2,1)S(1)} %add_convert_fusion.11.refs_11_), channel_id=1, source_target_pairs={{0,8},{4,12},{8,0},{12,4},{1,9},{5,13},{9,1},{13,5},{2,10},{6,14},... | collective-permute-start | bytes 835592 | tf_op jit(solution)/shard_map/ppermute | solution.py:277
  478.0 9.1 %collective-permute-start.132 = (bf16[272,512]{1,0:T(8,128)(2,1)S(1)}, bf16[272,512]{1,0:T(8,128)(2,1)S(1)}, u32[]{:S(2)}, u32[]{:S(2)}) collective-permute-start(bf16[272,512]{1,0:T(8,128)(2,1)S(1)} %add_convert_fusion.10.refs_6_.refs_10_), channel_id=1, source_target_pairs={{0,8},{4,12},{8,0},{12,4},{1,9},{5,13},{9,1},{13,5},{2,10},{6,14},... | collective-permute-start | bytes 835592 | tf_op jit(solution)/shard_map/ppermute | solution.py:277
  482.1 10.7 %collective-permute-start.138 = (bf16[272,512]{1,0:T(8,128)(2,1)S(1)}, bf16[272,512]{1,0:T(8,128)(2,1)S(1)}, u32[]{:S(2)}, u32[]{:S(2)}) collective-permute-start(bf16[272,512]{1,0:T(8,128)(2,1)S(1)} %get-tuple-element.435), channel_id=1, source_target_pairs={{16,0},{17,1},{18,2},{19,3},{20,4},{21,5},{22,6},{23,7},{24,8},{25... | collective-permute-start | bytes 835592 | tf_op jit(solution)/shard_map/ppermute | solution.py:295
  494.4 11.0 %collective-permute-start.134 = (bf16[272,512]{1,0:T(8,128)(2,1)S(1)}, bf16[272,512]{1,0:T(8,128)(2,1)S(1)}, u32[]{:S(2)}, u32[]{:S(2)}) collective-permute-start(bf16[272,512]{1,0:T(8,128)(2,1)S(1)} %get-tuple-element.432), channel_id=1, source_target_pairs={{16,0},{17,1},{18,2},{19,3},{20,4},{21,5},{22,6},{23,7},{24,8},{25... | collective-permute-start | bytes 835592 | tf_op jit(solution)/shard_map/ppermute | solution.py:295
  498.5 6.8 collective-permute-start.140
  505.4 9.1 %collective-permute-start.144 = (bf16[272,512]{1,0:T(8,128)(2,1)S(1)}, bf16[272,512]{1,0:T(8,128)(2,1)S(1)}, u32[]{:S(2)}, u32[]{:S(2)}) collective-permute-start(bf16[272,512]{1,0:T(8,128)(2,1)S(1)} %add_convert_fusion.7.refs_10_), channel_id=1, source_target_pairs={{0,8},{4,12},{8,0},{12,4},{1,9},{5,13},{9,1},{13,5},{2,10},{6,14},... | collective-permute-start | bytes 835592 | tf_op jit(solution)/shard_map/ppermute | solution.py:277
  514.8 9.1 %collective-permute-start.142 = (bf16[272,512]{1,0:T(8,128)(2,1)S(1)}, bf16[272,512]{1,0:T(8,128)(2,1)S(1)}, u32[]{:S(2)}, u32[]{:S(2)}) collective-permute-start(bf16[272,512]{1,0:T(8,128)(2,1)S(1)} %add_convert_fusion.6.refs_11_), channel_id=1, source_target_pairs={{0,8},{4,12},{8,0},{12,4},{1,9},{5,13},{9,1},{13,5},{2,10},{6,14},... | collective-permute-start | bytes 835592 | tf_op jit(solution)/shard_map/ppermute | solution.py:277
  572.5 246.1 %all-reduce.9.cloned.1.call-start = ((), (), s32[]{:S(2)}) async-start(), calls=%async_computation | async-start | bytes 4259840 | tf_op jit(solution)/shard_map/psum | solution.py:437
  592.7 9.5 %collective-permute-start.150 = (bf16[272,512]{1,0:T(8,128)(2,1)S(1)}, bf16[272,512]{1,0:T(8,128)(2,1)S(1)}, u32[]{:S(2)}, u32[]{:S(2)}) collective-permute-start(bf16[272,512]{1,0:T(8,128)(2,1)S(1)} %copy-done.87), channel_id=1, source_target_pairs={{0,8},{4,12},{8,0},{12,4},{1,9},{5,13},{9,1},{13,5},{2,10},{6,14},... | collective-permute-start | bytes 835592 | tf_op jit(solution)/shard_map/ppermute | solution.py:277
  594.0 20.8 %collective-permute-start.148 = (bf16[272,512]{1,0:T(8,128)(2,1)S(1)}, bf16[272,512]{1,0:T(8,128)(2,1)S(1)}, u32[]{:S(2)}, u32[]{:S(2)}) collective-permute-start(bf16[272,512]{1,0:T(8,128)(2,1)S(1)} %add_convert_fusion.2.refs_6_.refs_20_), channel_id=1, source_target_pairs={{0,8},{4,12},{8,0},{12,4},{1,9},{5,13},{9,1},{13,5},{2,10},{6,14},... | collective-permute-start | bytes 835592 | tf_op jit(solution)/shard_map/ppermute | solution.py:277
  602.2 24.9 %collective-permute-start.151 = (bf16[272,512]{1,0:T(8,128)(2,1)S(1)}, bf16[272,512]{1,0:T(8,128)(2,1)S(1)}, u32[]{:S(2)}, u32[]{:S(2)}) collective-permute-start(bf16[272,512]{1,0:T(8,128)(2,1)S(1)} %add_convert_fusion.refs_3_), channel_id=1, source_target_pairs={{0,4},{4,0},{8,12},{12,8},{1,5},{5,1},{9,13},{13,9},{2,6},{6,2},{1... | collective-permute-start | bytes 835592 | tf_op jit(solution)/shard_map/ppermute | solution.py:277
  614.8 15.5 %collective-permute-start.149 = (bf16[272,512]{1,0:T(8,128)(2,1)S(1)}, bf16[272,512]{1,0:T(8,128)(2,1)S(1)}, u32[]{:S(2)}, u32[]{:S(2)}) collective-permute-start(bf16[272,512]{1,0:T(8,128)(2,1)S(1)} %add_convert_fusion.1.refs_3_), channel_id=1, source_target_pairs={{0,4},{4,0},{8,12},{12,8},{1,5},{5,1},{9,13},{13,9},{2,6},{6,2},{1... | collective-permute-start | bytes 835592 | tf_op jit(solution)/shard_map/ppermute | solution.py:277
  (496 other events, 3935.2 us)
Sparse Core Ops, SparseCore 0:
  572.6 155.3 all-reduce.10
  731.1 87.3 all-reduce.8
